TPU v7x, 32 devices: a whole 2x2x4 slice. The times are simulated.
32 devices in a mesh: dp: 32 (over z, y, x, core).
Axes of the slice: x: 2, y: 2, z: 4, core: 2. Of those that a mesh axis runs over, the one named last changes fastest.
Arguments:
- block_in: bfloat16 [32, 1024, 1024], P('dp'), may hold values from -6 to 6
- condition: float32 [32, 1024], P('dp'), may hold values from -6 to 6
- out_grad: bfloat16 [32, 1024, 1024], P('dp'), may hold values from -6 to 6
- weights: float32 [1024, 18432], P('dp'), may hold values from -2 to 2, as said below
- biases: float32 [14336], P('dp'), may hold values from -0.75 to 0.75
- first_moment: float32 [1024, 18432], P('dp'), may hold values from -32 to 32
- second_moment: float32 [1024, 18432], P('dp'), may hold values from 131.072 to 983.04
- bias_first: float32 [14336], P('dp'), may hold values from -32 to 32
- bias_second: float32 [14336], P('dp'), may hold values from 131.072 to 983.04
Outputs:
- block_out: bfloat16 [32, 1024, 1024], P('dp')
- input_grad: float32 [32, 1024, 1024], P('dp')
- condition_grad: float32 [32, 1024], P('dp')
- weight_grad: float32 [1024, 18432], P('dp')
- bias_grad: float32 [14336], P('dp')
- new_weights: float32 [1024, 18432], P('dp')
- new_biases: float32 [14336], P('dp')
- new_first: float32 [1024, 18432], P('dp')
- new_second: float32 [1024, 18432], P('dp')
- new_bias_first: float32 [14336], P('dp')
- new_bias_second: float32 [14336], P('dp')
Inputs may be any that keep to these rules, and one draw needn't show every extreme that they name: `weights`: columns as described in the first step.
All inputs are finite; a program needn't handle non-finite values.
Results may differ from a plain program's by a relative error of at most 0.017.
The roundings to bfloat16 on the way count: a program that leaves them out, or rounds other values in their place, can miss the bound.
Values may be sent and summed in bfloat16 or wider, within the bound.
A program may use at most 320 MiB of HBM per device.

v0:
```python
import jax
import jax.numpy as jnp
from jax import lax
from jax.sharding import PartitionSpec as P

D = 1024
HEADS = 16
HEAD = 64
FF = 4096
STEP = 3


norm_eps = 1e-06
gelu_coef = 0.7978845608028654
learn_rate = 0.01
beta_first = 0.9
beta_second = 0.95
adam_eps = 1e-08
weight_decay = 0.05
contract_rows = (((0,), (0,)), ((), ()))
contract_cols = (((1,), (1,)), ((), ()))


def norm_rows(values):
    center = values - jnp.mean(values, axis=-1, keepdims=True)
    inv_std = lax.rsqrt(jnp.mean(center * center, axis=-1, keepdims=True) + norm_eps)
    return (center * inv_std, inv_std)


def norm_back(grad_hat, normed, inv_std):
    return inv_std * (
        grad_hat
        - jnp.mean(grad_hat, axis=-1, keepdims=True)
        - normed * jnp.mean(grad_hat * normed, axis=-1, keepdims=True)
    )


def gelu_pair(inner):
    tangent = jnp.tanh(gelu_coef * (inner + 0.044715 * inner * inner * inner))
    value = 0.5 * inner * (1.0 + tangent)
    slope = 0.5 * (1.0 + tangent) + 0.5 * inner * (1.0 - tangent * tangent) * gelu_coef * (
        1.0 + 3.0 * 0.044715 * inner * inner
    )
    return (value, slope)


def attend(query, keys, values):
    seq_len = query.shape[0]
    rows_per = min(512, seq_len)
    scale = HEAD ** (-0.5)
    key_heads = keys.reshape(seq_len, HEADS, HEAD)
    value_heads = values.reshape(seq_len, HEADS, HEAD)
    query_blocks = query.reshape(seq_len // rows_per, rows_per, HEADS, HEAD)

    def one_block(query_block):
        scores = (
            jnp.einsum("qhd,khd->hqk", query_block, key_heads, preferred_element_type=jnp.float32)
            * scale
        )
        row_max = jnp.max(scores, axis=-1, keepdims=True)
        log_total = row_max + jnp.log(jnp.sum(jnp.exp(scores - row_max), axis=-1, keepdims=True))
        probs = jnp.exp(scores - log_total).astype(jnp.bfloat16)
        mixed = jnp.einsum("hqk,khd->qhd", probs, value_heads, preferred_element_type=jnp.float32)
        return (mixed.astype(jnp.bfloat16).reshape(rows_per, HEADS * HEAD), log_total[..., 0])

    mixed, log_total = lax.map(one_block, query_blocks)
    return (mixed.reshape(seq_len, HEADS * HEAD), log_total)


def attend_back(query, keys, values, log_total, grad_mixed):
    seq_len = query.shape[0]
    rows_per = min(512, seq_len)
    block_count = seq_len // rows_per
    scale = HEAD ** (-0.5)
    key_heads = keys.reshape(seq_len, HEADS, HEAD)
    value_heads = values.reshape(seq_len, HEADS, HEAD)
    query_blocks = query.reshape(block_count, rows_per, HEADS, HEAD)
    grad_blocks = grad_mixed.reshape(block_count, rows_per, HEADS, HEAD)

    def one_block(carry, inputs):
        query_block, grad_block, total_block = inputs
        scores = (
            jnp.einsum("qhd,khd->hqk", query_block, key_heads, preferred_element_type=jnp.float32)
            * scale
        )
        probs = jnp.exp(scores - total_block[..., None])
        grad_probs = jnp.einsum(
            "qhd,khd->hqk", grad_block, value_heads, preferred_element_type=jnp.float32
        )
        grad_scores = (
            probs * (grad_probs - jnp.sum(probs * grad_probs, axis=-1, keepdims=True)) * scale
        ).astype(jnp.bfloat16)
        grad_query = jnp.einsum(
            "hqk,khd->qhd", grad_scores, key_heads, preferred_element_type=jnp.float32
        )
        grad_keys = carry[0] + jnp.einsum(
            "hqk,qhd->khd", grad_scores, query_block, preferred_element_type=jnp.float32
        )
        grad_values = carry[1] + jnp.einsum(
            "hqk,qhd->khd",
            probs.astype(jnp.bfloat16),
            grad_block,
            preferred_element_type=jnp.float32,
        )
        return ((grad_keys, grad_values), grad_query.reshape(rows_per, HEADS * HEAD))

    empty = jnp.zeros((seq_len, HEADS, HEAD), jnp.float32)
    (grad_keys, grad_values), grad_query = lax.scan(
        one_block, (empty, empty), (query_blocks, grad_blocks, log_total)
    )
    width = HEADS * HEAD
    return (
        grad_query.reshape(seq_len, width),
        grad_keys.reshape(seq_len, width),
        grad_values.reshape(seq_len, width),
    )


def forward_latent(tokens, mod_row, mats, bias_full):
    w_qkv, w_out, w_up, w_down = mats
    shift_one, scale_one, gate_one, shift_two, scale_two, gate_two = jnp.split(mod_row, 6)
    tokens_f = tokens.astype(jnp.float32)
    normed_one, inv_one = norm_rows(tokens_f)
    hidden_one = (normed_one * (1.0 + scale_one) + shift_one).astype(jnp.bfloat16)
    qkv_bias = jnp.concatenate([bias_full[0:D], jnp.zeros((D,), jnp.float32), bias_full[D : 2 * D]])
    qkv_all = (jnp.dot(hidden_one, w_qkv, preferred_element_type=jnp.float32) + qkv_bias).astype(
        jnp.bfloat16
    )
    query, keys, values = (qkv_all[:, :D], qkv_all[:, D : 2 * D], qkv_all[:, 2 * D :])
    mixed, log_total = attend(query, keys, values)
    branch = jnp.dot(mixed, w_out, preferred_element_type=jnp.float32) + bias_full[2 * D : 3 * D]
    middle = tokens_f + gate_one * branch
    normed_two, inv_two = norm_rows(middle)
    hidden_two = (normed_two * (1.0 + scale_two) + shift_two).astype(jnp.bfloat16)
    inner = (
        jnp.dot(hidden_two, w_up, preferred_element_type=jnp.float32)
        + bias_full[3 * D : 3 * D + FF]
    )
    value, slope = gelu_pair(inner)
    activ = value.astype(jnp.bfloat16)
    down = (
        lax.dot_general(activ, w_down, contract_cols, preferred_element_type=jnp.float32)
        + bias_full[3 * D + FF : 4 * D + FF]
    )
    result = (middle + gate_two * down).astype(jnp.bfloat16)
    saved = (
        normed_one,
        inv_one,
        hidden_one,
        query,
        keys,
        values,
        mixed,
        log_total,
        branch,
        normed_two,
        inv_two,
        hidden_two,
        slope,
        activ,
        down,
    )
    return (result, saved)


def backward_latent(grad_out, mod_row, saved, mats):
    w_qkv, w_out, w_up, w_down = mats
    (
        normed_one,
        inv_one,
        hidden_one,
        query,
        keys,
        values,
        mixed,
        log_total,
        branch,
        normed_two,
        inv_two,
        hidden_two,
        slope,
        activ,
        down,
    ) = saved
    shift_one, scale_one, gate_one, shift_two, scale_two, gate_two = jnp.split(mod_row, 6)
    grad_f = grad_out.astype(jnp.float32)
    grad_down = grad_f * gate_two
    grad_gate_two = jnp.sum(grad_f * down, axis=0)
    down_b = grad_down.astype(jnp.bfloat16)
    grad_w_down = lax.dot_general(down_b, activ, contract_rows, preferred_element_type=jnp.float32)
    grad_inner = jnp.dot(down_b, w_down, preferred_element_type=jnp.float32) * slope
    inner_b = grad_inner.astype(jnp.bfloat16)
    grad_w_up = lax.dot_general(
        hidden_two, inner_b, contract_rows, preferred_element_type=jnp.float32
    )
    grad_hidden_two = lax.dot_general(
        inner_b, w_up, contract_cols, preferred_element_type=jnp.float32
    )
    grad_shift_two = jnp.sum(grad_hidden_two, axis=0)
    grad_scale_two = jnp.sum(grad_hidden_two * normed_two, axis=0)
    grad_middle = grad_f + norm_back(grad_hidden_two * (1.0 + scale_two), normed_two, inv_two)
    grad_branch = grad_middle * gate_one
    grad_gate_one = jnp.sum(grad_middle * branch, axis=0)
    branch_b = grad_branch.astype(jnp.bfloat16)
    grad_w_out = lax.dot_general(mixed, branch_b, contract_rows, preferred_element_type=jnp.float32)
    grad_mixed = lax.dot_general(
        branch_b, w_out, contract_cols, preferred_element_type=jnp.float32
    ).astype(jnp.bfloat16)
    grad_query, grad_keys, grad_values = attend_back(query, keys, values, log_total, grad_mixed)
    qkv_b = jnp.concatenate([grad_query, grad_keys, grad_values], axis=1).astype(jnp.bfloat16)
    grad_w_qkv = lax.dot_general(
        hidden_one, qkv_b, contract_rows, preferred_element_type=jnp.float32
    )
    grad_hidden_one = lax.dot_general(
        qkv_b, w_qkv, contract_cols, preferred_element_type=jnp.float32
    )
    grad_shift_one = jnp.sum(grad_hidden_one, axis=0)
    grad_scale_one = jnp.sum(grad_hidden_one * normed_one, axis=0)
    grad_input = grad_middle + norm_back(grad_hidden_one * (1.0 + scale_one), normed_one, inv_one)
    grad_mod = jnp.concatenate(
        [
            grad_shift_one,
            grad_scale_one,
            grad_gate_one,
            grad_shift_two,
            grad_scale_two,
            grad_gate_two,
        ]
    )
    bias_row = jnp.concatenate(
        [
            jnp.sum(grad_query, axis=0),
            jnp.sum(grad_values, axis=0),
            jnp.sum(grad_branch, axis=0),
            jnp.sum(grad_inner, axis=0),
            jnp.sum(grad_down, axis=0),
            grad_mod,
        ]
    )
    return (grad_input, grad_mod, (grad_w_qkv, grad_w_out, grad_w_up, grad_w_down), bias_row)


def adam_step(param, grad, first, second, decay):
    new_first = beta_first * first + (1.0 - beta_first) * grad
    new_second = beta_second * second + (1.0 - beta_second) * grad * grad
    step_size = learn_rate / (1.0 - beta_first**STEP)
    denom = jnp.sqrt(new_second / (1.0 - beta_second**STEP)) + adam_eps
    new_param = param - step_size * new_first / denom - learn_rate * decay * param
    return (new_param, new_first, new_second)


def on_device(
    block_in,
    condition,
    out_grad,
    weights,
    biases,
    first_moment,
    second_moment,
    bias_first,
    bias_second,
):
    weights_b = weights.astype(jnp.bfloat16)
    local_qkv = weights_b[:, : 3 * D]
    local_out = weights_b[:, 3 * D : 4 * D]
    local_up = weights_b[:, 4 * D : 4 * D + FF]
    local_down = weights_b[:, 4 * D + FF : 4 * D + 2 * FF]
    local_ada = weights_b[:, 4 * D + 2 * FF :]
    cond_act = jax.nn.silu(condition).astype(jnp.bfloat16)
    w_qkv, w_out, w_up, w_down, bias_all = (
        lax.all_gather(local_qkv, "dp", axis=0, tiled=True),
        lax.all_gather(local_out, "dp", axis=0, tiled=True),
        lax.all_gather(local_up, "dp", axis=0, tiled=True),
        lax.all_gather(local_down, "dp", axis=0, tiled=True),
        lax.all_gather(biases.astype(jnp.bfloat16), "dp", axis=0, tiled=True),
    )
    bias_full = bias_all.astype(jnp.float32)
    ada_full = lax.all_gather(local_ada, "dp", axis=0, tiled=True)
    mod = jnp.dot(cond_act, ada_full, preferred_element_type=jnp.float32) + bias_full[4 * D + FF :]
    mats = (w_qkv, w_out, w_up, w_down)

    def forward_one(inputs):
        return forward_latent(inputs[0], inputs[1], mats, bias_full)

    block_out, saved = lax.map(forward_one, (block_in, mod))
    back_mats = (
        lax.all_gather(local_qkv, "dp", axis=0, tiled=True),
        lax.all_gather(local_out, "dp", axis=0, tiled=True),
        lax.all_gather(local_up, "dp", axis=0, tiled=True),
        lax.all_gather(local_down, "dp", axis=0, tiled=True),
    )

    def backward_one(carry, inputs):
        grad_out, mod_row, kept = inputs
        grad_input, grad_mod, grads, bias_row = backward_latent(grad_out, mod_row, kept, back_mats)
        summed = tuple((total + part for total, part in zip(carry[0], grads)))
        return ((summed, carry[1] + bias_row), (grad_input, grad_mod))

    init = (
        tuple((jnp.zeros(mat.shape, jnp.float32) for mat in back_mats)),
        jnp.zeros((10 * D + FF,), jnp.float32),
    )
    (grads, bias_part), (input_grad, grad_mod) = lax.scan(
        backward_one, init, (out_grad, mod, saved)
    )
    mod_b = grad_mod.astype(jnp.bfloat16)
    grad_qkv, grad_out_w, grad_up, grad_down, bias_grad = (
        lax.psum_scatter(grads[0], "dp", scatter_dimension=0, tiled=True),
        lax.psum_scatter(grads[1], "dp", scatter_dimension=0, tiled=True),
        lax.psum_scatter(grads[2], "dp", scatter_dimension=0, tiled=True),
        lax.psum_scatter(grads[3], "dp", scatter_dimension=0, tiled=True),
        lax.psum_scatter(bias_part, "dp", scatter_dimension=0, tiled=True),
    )
    ada_back = lax.all_gather(local_ada, "dp", axis=0, tiled=True)
    grad_ada = lax.psum_scatter(
        lax.dot_general(cond_act, mod_b, contract_rows, preferred_element_type=jnp.float32),
        "dp",
        scatter_dimension=0,
        tiled=True,
    )
    cond_act_grad = lax.dot_general(
        mod_b, ada_back, contract_cols, preferred_element_type=jnp.float32
    )
    sigma = jax.nn.sigmoid(condition)
    condition_grad = cond_act_grad * (sigma * (1.0 + condition * (1.0 - sigma)))
    weight_grad = jnp.concatenate([grad_qkv, grad_out_w, grad_up, grad_down, grad_ada], axis=1)
    new_weights, new_first, new_second = adam_step(
        weights, weight_grad, first_moment, second_moment, weight_decay
    )
    new_biases, new_bias_first, new_bias_second = adam_step(
        biases, bias_grad, bias_first, bias_second, 0.0
    )
    return (
        block_out,
        input_grad,
        condition_grad,
        weight_grad,
        bias_grad,
        new_weights,
        new_biases,
        new_first,
        new_second,
        new_bias_first,
        new_bias_second,
    )


def solution(mesh):
    placed = (
        P("dp", None, None),
        P("dp", None),
        P("dp", None, None),
        P("dp", None),
        P("dp"),
        P("dp", None),
        P("dp", None),
        P("dp"),
        P("dp"),
    )
    return jax.shard_map(
        on_device,
        mesh=mesh,
        in_specs=placed,
        out_specs=(
            P("dp", None, None),
            P("dp", None, None),
            P("dp", None),
            P("dp", None),
            P("dp"),
            P("dp", None),
            P("dp"),
            P("dp", None),
            P("dp", None),
            P("dp"),
            P("dp"),
        ),
        check_vma=False,
    )
```

profile of v0, /device:TPU:0, one launch (start us, length us, event | category | flops | bytes accessed | tf_op | source)
XLA Modules:
  0.0 1805.0 jit_solution(11278831886075476797)
XLA Ops:
  13.3 43.2 %all-reduce = bf16[14336]{0:T(1024)(128)(2,1)S(1)} all-reduce(bf16[14336]{0:T(1024)(128)(2,1)S(1)} %dynamic-update-slice), channel_id=1, replica_groups=mesh['dp'=32] {'dp'}, use_global_device_ids=true, to_apply=%add | all-reduce | flops 14336 | bytes 57344
  58.8 52.2 %all-gather.6.cloned.1.call-done = bf16[1024,6144]{1,0:T(8,128)(2,1)} async-done(((bf16[32,6144]{1,0:T(8,128)(2,1)}), bf16[1024,6144]{1,0:T(8,128)(2,1)}) %all-gather.6.cloned.1.call-update) | async-done | bytes 12582928 | tf_op jit(solution)/shard_map/all_gather | solution.py:278
  111.0 6.3 fusion.94
  117.9 64.3 %all-gather.8.cloned.1.call-done = bf16[1024,3072]{1,0:T(8,128)(2,1)} async-done(((bf16[32,3072]{1,0:T(8,128)(2,1)}), bf16[1024,3072]{1,0:T(8,128)(2,1)}) %all-gather.8.cloned.1.call-update) | async-done | bytes 6291472 | tf_op jit(solution)/shard_map/all_gather | solution.py:271
  182.2 10.1 add_convert_fusion
  199.2 5.4 copy.52
  211.4 95.4 %while.30 = (s32[]{:T(128)}, bf16[2,512,1024]{2,1,0:T(8,128)(2,1)}, f32[2,16,512]{2,1,0:T(8,128)S(1)}, bf16[2,512,16,64]{1,3,2,0:T(8,128)(2,1)}, bf16[1024,16,64...) while((s32[]{:T(128)}, bf16[2,512,1024]{2,1,0:T(8,128)(2,1)}, ...), condition=%wide.region_5.6_spmd, body=%wide.region_2.0_spmd.sunk | while | flops 2215108608 | bytes 111412304 | solution.py:66
  211.6 14.8 multiply_reduce_fusion.10
  226.5 14.3 exponential_reduce_fusion.2
  240.8 15.5 fusion.155
  258.7 14.8 multiply_reduce_fusion.10
  273.5 14.2 exponential_reduce_fusion.2
  287.8 16.5 fusion.155
  306.8 7.5 fusion.107
  318.9 21.9 %multiply_convert_fusion.1 = (bf16[1024,4096]{1,0:T(8,128)(2,1)}, f32[1024,4096]{1,0:T(8,128)}) fusion(f32[4096]{0:T(1024)S(1)} %copy-done.16, bf16[1024,4096]{1,0:T(8,128)(2,1)} %all-gather.12.cloned.1.call-done, f32[1024,1024]{1,0:T(8,128)} %copy-done.5, f32[1024]{0:T(1024)S(1)} %bitcast.184, f32[1024]{0:T(1024)S(1)} %bitcast.186, ...), kind=kOutput, calls=%fused_computation.57 | convolution fusion | flops 8637120512 | bytes 37781504 | tf_op jit(solution)/shard_map/while/body/eval_jaxpr/dot_general | solution.py:136
  340.8 57.5 %all-gather.14.cloned.1.call-done = bf16[1024,4096]{1,0:T(8,128)(2,1)} async-done(((bf16[32,4096]{1,0:T(8,128)(2,1)}), bf16[1024,4096]{1,0:T(8,128)(2,1)}) %all-gather.14.cloned.1.call-update) | async-done | bytes 8388624 | tf_op jit(solution)/shard_map/all_gather | solution.py:274
  398.3 26.1 %fusion.114 = (f32[4096]{0:T(1024)}, bf16[1024,4096]{1,0:T(8,128)(2,1)}) fusion(f32[1024,4096]{1,0:T(8,128)} %get-tuple-element.426, f32[4096]{0:T(1024)S(1)} %copy-done.16, bf16[1024,4096]{1,0:T(8,128)(2,1)} %all-gather.14.cloned.1.call-done, bf16[1,1024,1024]{2,1,0:T(8,128)(2,1)} %param.15, f32[1024]{0:T(1024)S(1)} %bitcast.181), kind=kOutput, calls=%fused_computation.171 | convolution fusion | flops 8681156608 | bytes 35688448 | tf_op jit(solution)/shard_map/while/body/eval_jaxpr/dot_general | solution.py:191
  424.4 16.9 multiply_reduce_fusion.2
  441.4 22.2 %fusion.66 = (f32[1024]{0:T(1024)}, f32[1024]{0:T(1024)}, bf16[1,1024,1024]{2,1,0:T(8,128)(2,1)}, f32[1024]{0:T(1024)}, f32[1024]{0:T(1024)}, /*index=5*/f32[1024,1024]{1,0:T(8,128)}) fusion(bf16[1,1024,1024]{2,1,0:T(8,128)(2,1)} %param.15, f32[1024]{0:T(1024)S(1)} %bitcast.182, f32[1024]{0:T(1024)S(1)} %copy-done.39, f32[1024,1024]{1,0:T(8,128)} %copy-done.5, ...), kind=kOutput, calls=%fused_computation.76 | convolution fusion | flops 8612999168 | bytes 37801984 | tf_op jit(solution)/shard_map/while/body/eval_jaxpr/dot_general | solution.py:142
  463.5 6.6 convolution_convert_fusion
  470.1 6.4 reshape.251
  476.5 5.4 copy.56
  481.9 356.7 %while.31 = (s32[]{:T(128)}, f32[1024,16,64]{0,2,1:T(8,128)}, f32[1024,16,64]{0,2,1:T(8,128)}, f32[2,512,1024]{1,2,0:T(8,128)}, bf16[2,512,16,64]{1,3,2,0:T(8,12...) while((s32[]{:T(128)}, f32[1024,16,64]{0,2,1:T(8,128)}, ...), condition=%wide.region_12.13_spmd.clone, body=%wide.region_10.12_spmd.clone.sunk | while | flops 5549082624 | bytes 352520384 | solution.py:108
  482.3 14.6 fusion.167
  496.9 13.2 fusion.166
  510.1 73.9 %fusion.168 = f32[16,512,64]{1,2,0:T(8,128)} fusion(bf16[1024,16,64]{0,2,1:T(8,128)(2,1)S(1)} %get-tuple-element.583, f32[16,512,1024]{2,1,0:T(8,128)} %fusion.166, f32[16,512,1024]{2,1,0:T(8,128)} %fusion.167, f32[16,512]{1,0:T(8,128)S(1)} %dynamic-slice_bitcast_fusion.2), kind=kOutput, calls=%fused_computation.24.clone.1 | convolution fusion | flops 1149248512 | bytes 71335936 | tf_op jit(solution)/shard_map/while/body/eval_jaxpr/while/body/eval_jaxpr/hqk,khd->qhd/dot_general | solution.py:93
  587.0 56.0 %bitcast_add_fusion.4 = f32[1024,16,64]{0,2,1:T(8,128)} fusion(f32[1024,16,64]{0,2,1:T(8,128)} %get-tuple-element.568, f32[16,512,1024]{2,1,0:T(8,128)} %fusion.166, f32[16,512,1024]{2,1,0:T(8,128)} %fusion.167, f32[16,512]{1,0:T(8,128)S(1)} %dynamic-slice_bitcast_fusion.2, pred[]{:T(512)S(6)} %compare.3, ...), kind=kOutput, calls=%fused_computation.27.clone.1 | convolution fusion | flops 1151345664 | bytes 143720960 | tf_op jit(solution)/shard_map/while/body/eval_jaxpr/while/body/eval_jaxpr/hqk,qhd->khd/dot_general | solution.py:96
  643.0 16.4 bitcast_add_fusion.5
  659.5 14.6 fusion.167
  674.0 13.2 fusion.166
  687.2 73.9 %fusion.168 = f32[16,512,64]{1,2,0:T(8,128)} fusion(bf16[1024,16,64]{0,2,1:T(8,128)(2,1)S(1)} %get-tuple-element.583, f32[16,512,1024]{2,1,0:T(8,128)} %fusion.166, f32[16,512,1024]{2,1,0:T(8,128)} %fusion.167, f32[16,512]{1,0:T(8,128)S(1)} %dynamic-slice_bitcast_fusion.2), kind=kOutput, calls=%fused_computation.24.clone.1 | convolution fusion | flops 1149248512 | bytes 71335936 | tf_op jit(solution)/shard_map/while/body/eval_jaxpr/while/body/eval_jaxpr/hqk,khd->qhd/dot_general | solution.py:93
  764.2 56.6 %bitcast_add_fusion.4 = f32[1024,16,64]{0,2,1:T(8,128)} fusion(f32[1024,16,64]{0,2,1:T(8,128)} %get-tuple-element.568, f32[16,512,1024]{2,1,0:T(8,128)} %fusion.166, f32[16,512,1024]{2,1,0:T(8,128)} %fusion.167, f32[16,512]{1,0:T(8,128)S(1)} %dynamic-slice_bitcast_fusion.2, pred[]{:T(512)S(6)} %compare.3, ...), kind=kOutput, calls=%fused_computation.27.clone.1 | convolution fusion | flops 1151345664 | bytes 143720960 | tf_op jit(solution)/shard_map/while/body/eval_jaxpr/while/body/eval_jaxpr/hqk,qhd->khd/dot_general | solution.py:96
  820.8 17.6 bitcast_add_fusion.5
  855.1 14.5 fusion.83
  870.2 7.2 fusion.93
  878.1 17.7 fusion.79
  896.5 15.7 fusion.88
  912.9 13.4 fusion.75
  926.4 11.7 broadcast_multiply_fusion
  940.8 40.4 %all-reduce.1 = f32[14336]{0:T(1024)S(1)} all-reduce(f32[14336]{0:T(1024)S(1)} %constant_dynamic-update-slice_fusion.18), channel_id=7, replica_groups=mesh['dp'=32] {'dp'}, use_global_device_ids=true, to_apply=%region_31.32.clone | all-reduce | flops 14336 | bytes 114688
  981.9 5.5 fusion.74
  987.4 8.5 convolution_multiply_fusion
  995.9 27.8 %reduce-scatter.6.cloned.1.call-done = f32[32,3072]{1,0:T(8,128)} async-done(((f32[1024,3072]{1,0:T(8,128)}), f32[32,3072]{1,0:T(8,128)}) %reduce-scatter.6.cloned.1.call-update) | async-done | bytes 393232 | tf_op jit(solution)/shard_map/reduce_scatter | solution.py:308
  1025.6 140.3 %reduce-scatter.8.cloned.1.call-done = f32[32,1024]{1,0:T(8,128)} async-done(((f32[1024,1024]{1,0:T(8,128)}), f32[32,1024]{1,0:T(8,128)}) %reduce-scatter.8.cloned.1.call-update) | async-done | bytes 131088 | tf_op jit(solution)/shard_map/reduce_scatter | solution.py:309
  1167.4 179.7 %reduce-scatter.10.cloned.1.call-done = f32[32,4096]{1,0:T(8,128)} async-done(((f32[1024,4096]{1,0:T(8,128)}), f32[32,4096]{1,0:T(8,128)}) %reduce-scatter.10.cloned.1.call-update) | async-done | bytes 524304 | tf_op jit(solution)/shard_map/reduce_scatter | solution.py:310
  1349.0 184.9 %reduce-scatter.12.cloned.1.call-done = f32[32,4096]{1,0:T(8,128)} async-done(((f32[1024,4096]{1,0:T(8,128)}), f32[32,4096]{1,0:T(8,128)}) %reduce-scatter.12.cloned.1.call-update) | async-done | bytes 524304 | tf_op jit(solution)/shard_map/reduce_scatter | solution.py:311
  1535.8 252.7 %reduce-scatter.14.cloned.1.call-done = f32[32,6144]{1,0:T(8,128)} async-done(((f32[1024,6144]{1,0:T(8,128)}), f32[32,6144]{1,0:T(8,128)}) %reduce-scatter.14.cloned.1.call-update) | async-done | bytes 786448 | tf_op jit(solution)/shard_map/reduce_scatter | solution.py:315
  1790.5 7.1 multiply_subtract_fusion
  (190 shorter events, 70.0 us)
Async XLA Ops:
  7.2 5.9 copy-start.23
  7.2 50.5 %copy-start.2 = (bf16[1,1024,1024]{2,1,0:T(8,128)(2,1)S(1)}, bf16[1,1024,1024]{2,1,0:T(8,128)(2,1)}, u32[]{:S(2)}) copy-start(bf16[1,1024,1024]{2,1,0:T(8,128)(2,1)} %param.13) | copy-start | bytes 6291460
  7.2 103.8 %all-gather.6.cloned.1.call-start = ((), (), s32[]{:S(2)}) async-start(), calls=%async_computation.5 | async-start | bytes 12976128 | tf_op jit(solution)/shard_map/all_gather | solution.py:278
  9.2 101.8 %copy-start.7 = (f32[1,1024]{1,0:T(1,128)S(1)}, f32[1,1024]{1,0:T(1,128)}, u32[]{:S(2)}) copy-start(f32[1,1024]{1,0:T(1,128)} %param.14) | copy-start | bytes 12292
  10.0 172.2 %all-gather.8.cloned.1.call-start = ((), (), s32[]{:S(2)}) async-start(), calls=%async_computation.6 | async-start | bytes 6488064 | tf_op jit(solution)/shard_map/all_gather | solution.py:271
  10.7 296.1 %all-gather.10.cloned.1.call-start = ((), (), s32[]{:S(2)}) async-start(), calls=%async_computation.7 | async-start | bytes 2162688 | tf_op jit(solution)/shard_map/all_gather | solution.py:272
  11.5 307.4 %all-gather.12.cloned.1.call-start = ((), (), s32[]{:S(2)}) async-start(), calls=%async_computation.8 | async-start | bytes 8650752 | tf_op jit(solution)/shard_map/all_gather | solution.py:273
  12.4 385.9 %all-gather.14.cloned.1.call-start = ((), (), s32[]{:S(2)}) async-start(), calls=%async_computation.9 | async-start | bytes 8650752 | tf_op jit(solution)/shard_map/all_gather | solution.py:274
  13.0 1010.8 %reduce-scatter.6.cloned.1.call-start = ((), (), s32[]{:S(2)}) async-start(), calls=%async_computation.10 | async-start | bytes 12976128 | tf_op jit(solution)/shard_map/reduce_scatter | solution.py:308
  58.0 124.2 %copy-start.9 = (f32[1024]{0:T(1024)}, f32[1024]{0:T(1024)S(1)}, u32[]{:S(2)}) copy-start(f32[1024]{0:T(1024)S(1)} %broadcast_multiply_fusion.6) | copy-start | bytes 12292
  58.8 123.4 %copy-start.13 = (f32[1024]{0:T(1024)}, f32[1024]{0:T(1024)S(1)}, u32[]{:S(2)}) copy-start(f32[1024]{0:T(1024)S(1)} %add_rsqrt_fusion.1) | copy-start | bytes 12292
  117.9 74.4 %copy-start.11 = (f32[1,1024]{1,0:T(1,128)}, f32[1,1024]{1,0:T(1,128)S(1)}, u32[]{:S(2)}) copy-start(f32[1,1024]{1,0:T(1,128)S(1)} %get-tuple-element.422) | copy-start | bytes 12292
  117.9 74.4 %copy-start.33 = (f32[1,1024]{1,0:T(1,128)}, f32[1,1024]{1,0:T(1,128)S(1)}, u32[]{:S(2)}) copy-start(f32[1,1024]{1,0:T(1,128)S(1)} %get-tuple-element.421) | copy-start | bytes 12292
  211.4 95.4 %copy-start.31 = (f32[1,1024]{1,0:T(1,128)S(1)}, f32[1,1024]{1,0:T(1,128)}, u32[]{:S(2)}) copy-start(f32[1,1024]{1,0:T(1,128)} %get-tuple-element.423) | copy-start | bytes 12292
  211.4 95.4 %copy-start.40 = (f32[1024]{0:T(1024)S(1)}, f32[1024]{0:T(1024)}, u32[]{:S(2)}) copy-start(f32[1024]{0:T(1024)} %get-tuple-element.415) | copy-start | bytes 12292
  314.3 2.0 copy-start.5
  314.3 4.5 copy-start.16
  314.4 4.5 copy-start.27
  314.4 4.5 copy-start.29
  314.4 127.0 %copy-start.21 = (f32[1024]{0:T(1024)}, f32[1024]{0:T(1024)S(1)}, u32[]{:S(2)}) copy-start(f32[1024]{0:T(1024)S(1)} %broadcast_multiply_fusion.5) | copy-start | bytes 12292
  316.9 124.4 %copy-start.37 = (f32[1024]{0:T(1024)}, f32[1024]{0:T(1024)S(1)}, u32[]{:S(2)}) copy-start(f32[1024]{0:T(1024)S(1)} %add_rsqrt_fusion) | copy-start | bytes 12292
  318.9 79.4 %copy-start.25 = (f32[1,1024]{1,0:T(1,128)S(1)}, f32[1,1024]{1,0:T(1,128)}, u32[]{:S(2)}) copy-start(f32[1,1024]{1,0:T(1,128)} %get-tuple-element.418) | copy-start | bytes 12292
  398.3 26.1 %copy-start.6 = (f32[1024,1024]{1,0:T(8,128)S(1)}, f32[1024,1024]{1,0:T(8,128)}, u32[]{:S(2)}) copy-start(f32[1024,1024]{1,0:T(8,128)} %copy-done.5) | copy-start | bytes 12582916
  424.4 17.0 copy-start.39
  482.3 14.6 copy-start
  482.3 14.6 copy-start.1
  659.5 14.6 copy-start
  659.5 14.6 copy-start.1
  850.2 4.8 copy-start.3
  850.2 4.8 copy-start.10
  850.2 4.8 copy-start.12
  850.2 4.8 copy-start.14
  850.3 4.8 copy-start.34
  869.5 296.3 %reduce-scatter.8.cloned.1.call-start = ((), (), s32[]{:S(2)}) async-start(), calls=%async_computation.11 | async-start | bytes 4325376 | tf_op jit(solution)/shard_map/reduce_scatter | solution.py:309
  877.4 469.7 %reduce-scatter.10.cloned.1.call-start = ((), (), s32[]{:S(2)}) async-start(), calls=%async_computation.12 | async-start | bytes 17301504 | tf_op jit(solution)/shard_map/reduce_scatter | solution.py:310
  895.8 638.1 %reduce-scatter.12.cloned.1.call-start = ((), (), s32[]{:S(2)}) async-start(), calls=%async_computation.13 | async-start | bytes 17301504 | tf_op jit(solution)/shard_map/reduce_scatter | solution.py:311
  912.2 876.3 %reduce-scatter.14.cloned.1.call-start = ((), (), s32[]{:S(2)}) async-start(), calls=%async_computation.14 | async-start | bytes 25952256 | tf_op jit(solution)/shard_map/reduce_scatter | solution.py:315
  912.9 13.4 copy-start.20
  912.9 13.4 copy-start.18
  912.9 13.4 copy-start.17
  912.9 13.4 copy-start.19
  938.1 2.6 copy-start.36
  938.1 2.6 copy-start.15
  938.1 2.6 copy-start.35
  938.1 43.1 %copy-start.24 = (f32[448]{0:T(512)S(1)}, f32[448]{0:T(512)}, u32[]{:S(2)}) copy-start(f32[448]{0:T(512)} %param.17) | copy-start | bytes 5380
  938.1 43.1 %copy-start.41 = (f32[448]{0:T(512)S(1)}, f32[448]{0:T(512)}, u32[]{:S(2)}) copy-start(f32[448]{0:T(512)} %param.20) | copy-start | bytes 5380
  938.1 43.1 %copy-start.42 = (f32[448]{0:T(512)S(1)}, f32[448]{0:T(512)}, u32[]{:S(2)}) copy-start(f32[448]{0:T(512)} %param.21) | copy-start | bytes 5380
  995.9 794.6 %copy-start.4 = (f32[32,18432]{1,0:T(8,128)S(1)}, f32[32,18432]{1,0:T(8,128)}, u32[]{:S(2)}) copy-start(f32[32,18432]{1,0:T(8,128)} %param.16) | copy-start | bytes 7077892
  (7 other events, 4.8 us)
Sparse Core Ops, SparseCore 0:
  11.5 99.4 all-gather.5
  114.4 67.7 all-gather.7
  185.1 54.8 all-gather.9
  242.7 76.1 all-gather.11
  322.2 76.0 all-gather.13
  869.7 154.0 reduce-scatter.5
  1026.2 139.6 reduce-scatter.7
  1168.2 178.8 reduce-scatter.9
  1349.6 184.2 reduce-scatter.11
  1541.3 247.1 reduce-scatter.13
where the time goes:
time: 1810 us; the launch traced here: 1800 us
  waiting for transfers between devices  962 us (53%)
  matrix products  606 us (33%)
  blocking collectives  83.5 us (5%)
  local copies, waits for them, and re-layouts  70.2 us (4%)
  other arithmetic  66.6 us (4%)
    reduce_scatter x1, waiting for transfers between devices, on_device(): lax.psum_scatter(lax.dot_general(cond_act, mod_b, contract_rows, preferre...  253 us
    reduce_scatter x1, waiting for transfers between devices, on_device(): lax.psum_scatter(grads[3], 'dp', scatter_dimension=0, tiled=True)  185 us
    reduce_scatter x1, waiting for transfers between devices, on_device(): lax.psum_scatter(grads[2], 'dp', scatter_dimension=0, tiled=True)  180 us
    dot_general x2, matrix products, one_block(): jnp.einsum('hqk,khd->qhd', grad_scores, key_heads, preferred_element_type...  148 us
    reduce_scatter x1, waiting for transfers between devices, on_device(): lax.psum_scatter(grads[1], 'dp', scatter_dimension=0, tiled=True)  140 us
    dot_general x2, matrix products, one_block(): jnp.einsum('hqk,qhd->khd', grad_scores, query_block, preferred_element_ty...  113 us
    unnamed x2, blocking collectives  83.5 us
    all_gather x1, waiting for transfers between devices, on_device(): lax.all_gather(local_qkv, 'dp', axis=0, tiled=True)  64.3 us
  transfers between devices with their start and end apart: 10, of which 9 were waited for; matrix products, arithmetic and copies ran while one was open for 14% of the time, Pallas kernels for 0%

commit v1 on v0

v1 whole, which is shorter than its diff:
```python
import functools

import jax
import jax.numpy as jnp
from jax import lax
from jax.experimental import pallas as pl
from jax.experimental.pallas import tpu as pltpu
from jax.sharding import PartitionSpec as P

D = 1024
FF = 4096
S = 1024
STEP = 3
CH = 512
NJ = FF // CH
learn_rate = 0.01
beta_first = 0.9
beta_second = 0.95
adam_eps = 1e-08
weight_decay = 0.05
gc = 0.7978845608028654
LOG2E = 1.4426950408889634
f32 = jnp.float32
bf = jnp.bfloat16
NT = (((1,), (1,)), ((), ()))
TN = (((0,), (0,)), ((), ()))
V = pl.BlockSpec(memory_space=pltpu.VMEM)
A = pl.BlockSpec(memory_space=pl.ANY)
sd = jax.ShapeDtypeStruct


def dot(a,b,dn=None):
    if dn is None: return jnp.dot(a,b,preferred_element_type=f32)
    return lax.dot_general(a,b,dn,preferred_element_type=f32)

def lane_half(x, hh):
    lane=lax.broadcasted_iota(jnp.int32, x.shape, 1)
    keep=(lane<64) if hh==0 else (lane>=64)
    return jnp.where(keep, x, jnp.zeros_like(x))

def gelu_pair(u):
    u2=u*u
    t=jnp.tanh(gc*(u+0.044715*u2*u))
    return 0.5*u*(1.0+t), 0.5*(1.0+t)+0.5*u*(1.0-t*t)*gc*(1.0+3.0*0.044715*u2)
def nrm(v):
    c=v-jnp.mean(v,axis=-1,keepdims=True)
    r=lax.rsqrt(jnp.mean(c*c,axis=-1,keepdims=True)+1e-6)
    return c*r,r
def rows_loop(n, R, f):
    def body(i,_):
        f(pl.ds(pl.multiple_of(i*R,R),R)); return 0
    lax.fori_loop(0,n//R,body,0)

def kb_kernel(R, tok, gout, attnT, mod, bias, bup, wout_h, wup_h, wdn_h,
      bo_ref, dx1_ref, dat_ref, dw_h, dwout_ref, dmod_ref, db_ref, dbup_ref,
      h2, h2T, dzb, dzT, z, dh2, o_s, wout, wbuf, act, du, dwst, wsem, osem, wosem):
    pltpu.make_async_copy(wout_h, wout, wosem).start()
    def fetch(j, slot):
        pltpu.make_async_copy(wup_h.at[j], wbuf.at[slot,0], wsem.at[slot,0]).start()
        pltpu.make_async_copy(wdn_h.at[j], wbuf.at[slot,1], wsem.at[slot,1]).start()
    fetch(0,0)
    shift1=mod[0:1];scale1=mod[1:2];gate1=mod[2:3];shift2=mod[3:4];scale2=mod[4:5];gate2=mod[5:6]
    db_ref[...]=jnp.zeros_like(db_ref); dmod_ref[...]=jnp.zeros_like(dmod_ref)
    pltpu.make_async_copy(wout_h, wout, wosem).wait()
    def pre(r):
        o=dot(attnT[:,r],wout[...],TN)+bias[2:3]
        o_s[r,:]=o
        x1=tok[r,:].astype(f32)+gate1*o
        xh,_=nrm(x1)
        h2[r,:]=(xh*(1.0+scale2)+shift2).astype(bf)
        dz=gout[r,:].astype(f32)*gate2
        dzb[r,:]=dz.astype(bf)
        db_ref[3:4]+=jnp.sum(dz,axis=0,keepdims=True)
    rows_loop(S,256,pre)
    for i in range(4):
        r=slice(i*256,(i+1)*256)
        h2T[:,r]=h2[r,:].T
        dzT[:,r]=dzb[r,:].T
    z[...]=jnp.zeros_like(z); dh2[...]=jnp.zeros_like(dh2)
    def chunk(j,_):
        slot=lax.rem(j,2)
        @pl.when(j+1<NJ)
        def _(): fetch(j+1,1-slot)
        pltpu.make_async_copy(wup_h.at[j], wbuf.at[slot,0], wsem.at[slot,0]).wait()
        pltpu.make_async_copy(wdn_h.at[j], wbuf.at[slot,1], wsem.at[slot,1]).wait()
        dbup_ref[j]=jnp.zeros((1,CH),f32)
        def row(r):
            u=dot(h2[r,:],wbuf[slot,0])+bup[j]
            a,sl=gelu_pair(u)
            ab=a.astype(bf); act[r,:]=ab
            da=dot(dzb[r,:],wbuf[slot,1])
            d=da*sl
            dbup_ref[j]+=jnp.sum(d,axis=0,keepdims=True)
            db_=d.astype(bf); du[r,:]=db_
            z[r,:]+=dot(ab,wbuf[slot,1],NT)
            dh2[r,:]+=dot(db_,wbuf[slot,0],NT)
        rows_loop(S,R,row)
        @pl.when(j>=2)
        def _():
            pltpu.make_async_copy(dwst.at[slot], dw_h.at[j], osem.at[slot]).wait()
        def wrow(r):
            dwst[slot,0,r,:]=dot(h2T[r,:],du[...])
            dwst[slot,1,r,:]=dot(dzT[r,:],act[...])
        rows_loop(D,256,wrow)
        pltpu.make_async_copy(dwst.at[slot], dw_h.at[j], osem.at[slot]).start()
        return 0
    lax.fori_loop(0,NJ,chunk,0)
    for s in range(2): pltpu.make_async_copy(dwst.at[s], dw_h.at[s], osem.at[s]).wait()
    def post(r):
        g=gout[r,:].astype(f32); o=o_s[r,:]
        x1=tok[r,:].astype(f32)+gate1*o
        xh,rstd=nrm(x1)
        zz=z[r,:]+bias[3:4]
        bo_ref[r,:]=(x1+gate2*zz).astype(bf)
        dmod_ref[5:6]+=jnp.sum(g*zz,axis=0,keepdims=True)
        dh=dh2[r,:]
        dmod_ref[3:4]+=jnp.sum(dh,axis=0,keepdims=True)
        dmod_ref[4:5]+=jnp.sum(dh*xh,axis=0,keepdims=True)
        gg=dh*(1.0+scale2)
        dx1=g+rstd*(gg-jnp.mean(gg,axis=-1,keepdims=True)-xh*jnp.mean(gg*xh,axis=-1,keepdims=True))
        dx1_ref[r,:]=dx1
        dmod_ref[2:3]+=jnp.sum(dx1*o,axis=0,keepdims=True)
        do=dx1*gate1
        db_ref[2:3]+=jnp.sum(do,axis=0,keepdims=True)
        dob=do.astype(bf)
        dzb[r,:]=dob
        t=dot(dob,wout[...],NT).astype(bf)
        for g4 in range(4): dat_ref[g4,r,:]=t[:,g4*256:(g4+1)*256]
    rows_loop(S,128,post)
    def wo(r):
        dwout_ref[r,:]=dot(attnT[r,:],dzb[...])
    rows_loop(D,256,wo)

def kb(R,*a):
    V=pl.BlockSpec(memory_space=pltpu.VMEM); A=pl.BlockSpec(memory_space=pl.ANY)
    sd=jax.ShapeDtypeStruct
    return pl.pallas_call(functools.partial(kb_kernel,R),
      out_shape=(sd((S,D),bf),sd((S,D),f32),sd((4,S,256),bf),sd((NJ,2,D,CH),f32),sd((D,D),f32),sd((8,D),f32),sd((8,D),f32),sd((NJ,1,CH),f32)),
      in_specs=[V]*6+[A]*3, out_specs=[V,V,V,A,V,V,V,V],
      scratch_shapes=[pltpu.VMEM((S,D),bf)]*4+[pltpu.VMEM((S,D),f32)]*3+[pltpu.VMEM((D,D),bf),pltpu.VMEM((2,2,D,CH),bf),pltpu.VMEM((S,CH),bf),pltpu.VMEM((S,CH),bf),
         pltpu.VMEM((2,2,D,CH),f32),pltpu.SemaphoreType.DMA((2,2)),pltpu.SemaphoreType.DMA((2,)),pltpu.SemaphoreType.DMA],
      compiler_params=pltpu.CompilerParams(vmem_limit_bytes=62*2**20), name=f"kb{R}")(*a)

def ka_kernel(QB, tok, mod, bqkv, w_h, qkv, attnT, lse, h1T, h1, wbuf, wsem):
    c=LOG2E/8.0
    def cp(g,slot): return pltpu.make_async_copy(w_h.at[g], wbuf.at[slot], wsem.at[slot])
    cp(0,0).start()
    shift1=mod[0:1]; scale1=mod[1:2]
    def ln(r):
        xh,_=nrm(tok[r,:].astype(f32))
        h1[r,:]=(xh*(1.0+scale1)+shift1).astype(bf)
    rows_loop(S,128,ln)
    for i in range(4):
        r=slice(i*256,(i+1)*256); h1T[:,r]=h1[r,:].T
    def group(g,_):
        slot=lax.rem(g,2)
        @pl.when(g<3)
        def _(): cp(g+1,1-slot).start()
        cp(g,slot).wait()
        def proj(r):
            qkv[g,r,:]=(dot(h1[r,:],wbuf[slot])+bqkv[g]).astype(bf)
        rows_loop(S,256,proj)
        for p in range(2):
            kp=qkv[g,:,256+p*128:256+(p+1)*128]; vp=qkv[g,:,512+p*128:512+(p+1)*128]
            ks=[lane_half(kp,h) for h in range(2)]; vT=vp.T
            for i in range(S//QB):
                q=qkv[g,i*QB:(i+1)*QB,p*128:(p+1)*128]
                for h in range(2):
                    s=dot(ks[h],q,NT)
                    m=jnp.max(s,axis=0,keepdims=True)
                    e=jnp.exp2((s-m)*c)
                    l=jnp.sum(e,axis=0,keepdims=True)
                    pr=(e*(1.0/l)).astype(bf)
                    o=dot(vT[h*64:(h+1)*64],pr)
                    lse[g,p*2+h:p*2+h+1,i*QB:(i+1)*QB]=m*0.125+jnp.log(l)
                    attnT[pl.ds(pl.multiple_of(g*256+(p*128+h*64),64),64),i*QB:(i+1)*QB]=o.astype(bf)
        return 0
    lax.fori_loop(0,4,group,0)
def ka(QB,*a):
    return pl.pallas_call(functools.partial(ka_kernel,QB),
      out_shape=(sd((4,S,768),bf),sd((D,S),bf),sd((4,4,S),f32),sd((D,S),bf)),
      in_specs=[V,V,V,A], out_specs=[V]*4,
      scratch_shapes=[pltpu.VMEM((S,D),bf),pltpu.VMEM((2,D,768),bf),pltpu.SemaphoreType.DMA((2,))],
      compiler_params=pltpu.CompilerParams(vmem_limit_bytes=60*2**20), name=f"ka{QB}")(*a)
def kc_kernel(QB, tok, mod, qkv, dat, lse, dx1, h1T, w_h, ig, dw_h, dmod, dbq, dqkv, dk_s, dv_s, dqT_s, dh1, wbuf, dwst, wsem, osem):
    c=LOG2E/8.0
    def cp(g,slot): return pltpu.make_async_copy(w_h.at[g], wbuf.at[slot], wsem.at[slot])
    def co(g,slot): return pltpu.make_async_copy(dwst.at[slot], dw_h.at[g], osem.at[slot])
    cp(0,0).start()
    dh1[...]=jnp.zeros_like(dh1); dmod[...]=jnp.zeros_like(dmod); dbq[...]=jnp.zeros_like(dbq)
    def group(g,_):
        slot=lax.rem(g,2)
        @pl.when(g<3)
        def _(): cp(g+1,1-slot).start()
        for p in range(2):
            sl=slice(p*128,(p+1)*128); slk=slice(256+p*128,256+(p+1)*128); slv=slice(512+p*128,512+(p+1)*128)
            kp=qkv[g,:,slk]; vp=qkv[g,:,slv]
            ks=[lane_half(kp,h) for h in range(2)]; vs=[lane_half(vp,h) for h in range(2)]
            kT=kp.T
            dk_s[...]=jnp.zeros_like(dk_s); dv_s[...]=jnp.zeros_like(dv_s)
            def qblk(i,_):
                r=pl.ds(pl.multiple_of(i*QB,QB),QB)
                q=qkv[g,r,sl]; da=dat[g,r,sl]
                for h in range(2):
                    s=dot(ks[h],q,NT)
                    pT=jnp.exp2(s*c-lse[g,p*2+h:p*2+h+1,r]*LOG2E)
                    dp=dot(vs[h],da,NT)
                    delta=jnp.sum(pT*dp,axis=0,keepdims=True)
                    ds=(pT*(dp-delta)).astype(bf)
                    dv_s[...]+=dot(pT.astype(bf),lane_half(da,h))
                    dk_s[...]+=dot(ds,lane_half(q,h))
                    dqT_s[h*64:(h+1)*64,r]=dot(kT[h*64:(h+1)*64],ds)
                return 0
            lax.fori_loop(0,S//QB,qblk,0)
            dq=dqT_s[...].T*0.125
            dbq[g,:,sl]=jnp.sum(dq,axis=0,keepdims=True)
            dqkv[:,sl]=dq.astype(bf)
            dqkv[:,slk]=(dk_s[...]*0.125).astype(bf)
            dbq[g,:,slv]=jnp.sum(dv_s[...],axis=0,keepdims=True)
            dqkv[:,slv]=dv_s[...].astype(bf)
        cp(g,slot).wait()
        @pl.when(g>=2)
        def _(): co(g,slot).wait()
        def wrow(r):
            dwst[slot,r,:]=dot(h1T[r,:],dqkv[...])
            dh1[r,:]+=dot(dqkv[r,:],wbuf[slot],NT)
        rows_loop(D,256,wrow)
        co(g,slot).start()
        return 0
    lax.fori_loop(0,4,group,0)
    for s_ in range(2): co(s_,s_).wait()
    scale1=mod[1:2]
    def post(r):
        xh,rstd=nrm(tok[r,:].astype(f32))
        dh=dh1[r,:]
        dmod[0:1]+=jnp.sum(dh,axis=0,keepdims=True)
        dmod[1:2]+=jnp.sum(dh*xh,axis=0,keepdims=True)
        gg=dh*(1.0+scale1)
        ig[r,:]=dx1[r,:]+rstd*(gg-jnp.mean(gg,axis=-1,keepdims=True)-xh*jnp.mean(gg*xh,axis=-1,keepdims=True))
    rows_loop(S,128,post)
def kc(QB,*a):
    return pl.pallas_call(functools.partial(kc_kernel,QB),
      out_shape=(sd((S,D),f32),sd((4,D,768),f32),sd((8,D),f32),sd((4,1,768),f32)),
      in_specs=[V]*7+[A], out_specs=[V,A,V,V],
      scratch_shapes=[pltpu.VMEM((S,768),bf),pltpu.VMEM((S,128),f32),pltpu.VMEM((S,128),f32),pltpu.VMEM((128,S),f32),pltpu.VMEM((S,D),f32),
        pltpu.VMEM((2,D,768),bf),pltpu.VMEM((2,D,768),f32),pltpu.SemaphoreType.DMA((2,)),pltpu.SemaphoreType.DMA((2,))],
      compiler_params=pltpu.CompilerParams(vmem_limit_bytes=60*2**20), name=f"kc{QB}")(*a)

def adam_step(param, grad, first, second, decay):
    new_first = beta_first * first + (1.0 - beta_first) * grad
    new_second = beta_second * second + (1.0 - beta_second) * grad * grad
    step_size = learn_rate / (1.0 - beta_first**STEP)
    denom = jnp.sqrt(new_second / (1.0 - beta_second**STEP)) + adam_eps
    new_param = param - step_size * new_first / denom - learn_rate * decay * param
    return (new_param, new_first, new_second)


def on_device(n, block_in, condition, out_grad, weights, biases, first_moment, second_moment, bias_first, bias_second):
    me = lax.axis_index("dp")
    rows = D // n
    wb = weights.astype(bf)
    qkv_l = wb[:, : 3 * D].reshape(rows, 3, 4, 256).transpose(2, 0, 1, 3).reshape(4, rows, 768)
    up_l = wb[:, 4 * D : 4 * D + FF].reshape(rows, NJ, CH).transpose(1, 0, 2)
    dn_l = wb[:, 4 * D + FF : 4 * D + 2 * FF].reshape(rows, NJ, CH).transpose(1, 0, 2)
    ada_l = wb[:, 4 * D + 2 * FF :]
    bias_full = lax.all_gather(biases.astype(bf), "dp", axis=0, tiled=True).astype(f32)
    cond_act = jax.nn.silu(condition).astype(bf)
    cond_all = lax.all_gather(cond_act, "dp", axis=0, tiled=True)
    cond_cols = lax.dynamic_slice_in_dim(cond_all, me * rows, rows, 1)
    mod_part = jnp.dot(cond_cols, ada_l, preferred_element_type=f32)
    mod = lax.psum_scatter(mod_part, "dp", scatter_dimension=0, tiled=True) + bias_full[4 * D + FF :]
    mod = jnp.concatenate([mod.reshape(6, D), jnp.zeros((2, D), f32)], axis=0)
    w_qkv = lax.all_gather(qkv_l, "dp", axis=1, tiled=True)
    w_out = lax.all_gather(wb[:, 3 * D : 4 * D], "dp", axis=0, tiled=True)
    w_up = lax.all_gather(up_l, "dp", axis=1, tiled=True)
    w_dn = lax.all_gather(dn_l, "dp", axis=1, tiled=True)
    zrow = jnp.zeros((D,), f32)
    bqkv = jnp.stack([bias_full[:D], zrow, bias_full[D : 2 * D]]).reshape(3, 4, 256).transpose(1, 0, 2).reshape(4, 1, 768)
    brows = jnp.stack([zrow, zrow, bias_full[2 * D : 3 * D], bias_full[3 * D + FF : 4 * D + FF], zrow, zrow, zrow, zrow])
    bup = bias_full[3 * D : 3 * D + FF].reshape(NJ, 1, CH)
    tok = block_in[0]
    gout = out_grad[0]
    qkv, attn_t, lse, h1t = ka(1024, tok, mod, bqkv, w_qkv)
    bo, dx1, dat, dw_mlp, dw_out, dmod_b, db, db_up = kb(512, tok, gout, attn_t, mod, brows, bup, w_out, w_up, w_dn)
    ig, dw_qkv, dmod_a, db_qkv = kc(1024, tok, mod, qkv, dat, lse, dx1, h1t, w_qkv)
    dmod = (dmod_a + dmod_b)[:6].reshape(1, 6 * D)
    g_mlp = lax.psum_scatter(dw_mlp, "dp", scatter_dimension=2, tiled=True)
    g_out = lax.psum_scatter(dw_out, "dp", scatter_dimension=0, tiled=True)
    g_qkv = lax.psum_scatter(dw_qkv, "dp", scatter_dimension=1, tiled=True)
    db_qkv = db_qkv.reshape(4, 3, 256).transpose(1, 0, 2).reshape(3, D)
    bias_row = jnp.concatenate([db_qkv[0], db_qkv[2], db[2], db_up.reshape(FF), db[3], dmod[0]])
    bias_grad = lax.psum_scatter(bias_row, "dp", scatter_dimension=0, tiled=True)
    dmod_all = lax.all_gather(dmod.astype(bf), "dp", axis=0, tiled=True)
    g_ada = lax.dot_general(cond_cols, dmod_all, TN, preferred_element_type=f32)
    cond_part = lax.dot_general(dmod_all, ada_l, NT, preferred_element_type=f32)
    cond_grad = lax.all_to_all(cond_part, "dp", split_axis=0, concat_axis=1, tiled=True)
    sigma = jax.nn.sigmoid(condition)
    cond_grad = cond_grad * (sigma * (1.0 + condition * (1.0 - sigma)))
    g_qkv = g_qkv.reshape(4, rows, 3, 256).transpose(1, 2, 0, 3).reshape(rows, 3 * D)
    g_mlp = g_mlp.transpose(2, 1, 0, 3).reshape(rows, 2 * FF)
    weight_grad = jnp.concatenate([g_qkv, g_out, g_mlp, g_ada], axis=1)
    new_weights, new_first, new_second = adam_step(weights, weight_grad, first_moment, second_moment, weight_decay)
    new_biases, new_bias_first, new_bias_second = adam_step(biases, bias_grad, bias_first, bias_second, 0.0)
    return (bo[None], ig[None], cond_grad, weight_grad, bias_grad, new_weights, new_biases, new_first, new_second, new_bias_first, new_bias_second)


def solution(mesh):
    three, two, one = P("dp", None, None), P("dp", None), P("dp")
    return jax.shard_map(
        functools.partial(on_device, mesh.shape["dp"]),
        mesh=mesh,
        in_specs=(three, two, three, two, one, two, two, one, one),
        out_specs=(three, three, two, two, one, two, one, two, two, one, one),
        check_vma=False,
    )
```

time: 1810 us -> 1320 us (0.73)
  matrix products: 606 us -> 3.36 us
  Pallas kernels: 0 us -> 215 us
  blocking collectives: 83.5 us -> 167 us
  waiting for transfers between devices: 962 us -> 891 us
  local copies, waits for them, and re-layouts: 70.2 us -> 12.1 us
  other arithmetic: 66.6 us -> 12 us
    dot_general x28 -> x3, matrix products: 606 us -> 3.36 us  [the longest x1 1.25 us: on_device(): g_ada = lax.dot_general(cond_cols, dmod_all, TN, preferred_element_type=f32)]
    reduce_scatter x5 -> x3, waiting for transfers between devices: 785 us -> 561 us  [the longest x1 353 us: on_device(): g_mlp = lax.psum_scatter(dw_mlp, 'dp', scatter_dimension=2, tiled=True)]
    pallas_call x0 -> x3, Pallas kernels: none -> 215 us  [the longest x1 95.3 us: kb(): pl.pallas_call(functools.partial(kb_kernel, R), out_shape=(sd((S, D), bf)...]
    all_gather x0 -> x2, blocking collectives: none -> 84.9 us  [the longest x1 43.6 us: on_device(): cond_all = lax.all_gather(cond_act, 'dp', axis=0, tiled=True)]
    unnamed x10 -> x9, waiting for transfers between devices: 0.72 us -> 83.3 us
    all_gather x5 -> x4, waiting for transfers between devices: 176 us -> 247 us  [the longest x1 80.5 us: on_device(): w_up = lax.all_gather(up_l, 'dp', axis=1, tiled=True)]
    reduce_sum x7 -> x0, other arithmetic: 36.5 us -> none  [the longest x2 28.5 us: one_block(): jnp.sum(jnp.exp(scores - row_max), axis=-1, keepdims=True)]
  transfers between devices with their start and end apart: 10 -> 9, of which waited for: 9 -> 8; matrix products, arithmetic and copies ran while one was open for 14% -> 1% of each run, Pallas kernels for 0% -> 3%
where the time goes in v1:
time: 1320 us
  waiting for transfers between devices  891 us (68%)
  Pallas kernels  215 us (16%)
  blocking collectives  167 us (13%)
  between operations  14.5 us (1%)
    reduce_scatter x1, waiting for transfers between devices, on_device(): g_mlp = lax.psum_scatter(dw_mlp, 'dp', scatter_dimension=2, tiled=True)  353 us
    reduce_scatter x1, waiting for transfers between devices, on_device(): g_out = lax.psum_scatter(dw_out, 'dp', scatter_dimension=0, tiled=True)  148 us
    pallas_call x1, Pallas kernels, kb(): pl.pallas_call(functools.partial(kb_kernel, R), out_shape=(sd((S, D), bf)...  95.3 us
    unnamed x9, waiting for transfers between devices  83.3 us
    unnamed x2, blocking collectives  82.1 us
    all_gather x1, waiting for transfers between devices, on_device(): w_up = lax.all_gather(up_l, 'dp', axis=1, tiled=True)  80.5 us
    all_gather x1, waiting for transfers between devices, on_device(): w_dn = lax.all_gather(dn_l, 'dp', axis=1, tiled=True)  80.1 us
    pallas_call x1, Pallas kernels, kc(): pl.pallas_call(functools.partial(kc_kernel, QB), out_shape=(sd((S, D), f3...  76.3 us
  transfers between devices with their start and end apart: 9, of which 8 were waited for; matrix products, arithmetic and copies ran while one was open for 1% of the time, Pallas kernels for 3%

profile of v1, /device:TPU:0, one launch (start us, length us, event | category | flops | bytes accessed | tf_op | source)
XLA Modules:
  0.0 1317.7 jit_solution(17614028340610211387)
XLA Ops:
  7.2 0.7 convert_bitcast_fusion
  7.9 43.6 %all-gather = bf16[32,1,1024]{2,1,0:T(2,128)(2,1)S(1)} all-gather(bf16[1,1,1024]{2,1,0:T(2,128)(2,1)S(1)} %get-tuple-element.53), channel_id=1, replica_groups=mesh['dp'=32] {'dp'}, dimensions={0}, use_global_device_ids=true | all-gather | bytes 67584 | tf_op jit(solution)/shard_map/all_gather | solution.py:268
  51.5 1.8 convert_element_type.27
  53.3 0.1 constant_dynamic-slice_fusion
  53.4 1.1 fusion.6
  54.6 0.1 reshape.109
  54.8 0.1 copy.69
  54.9 0.9 reshape.110
  55.9 0.6 slice.103
  56.6 0.7 copy.68
  57.4 0.7 copy.67
  58.3 0.3 dynamic-update-slice
  58.5 37.4 %all-reduce.1 = bf16[14336]{0:T(1024)(128)(2,1)S(1)} all-reduce(bf16[14336]{0:T(1024)(128)(2,1)S(1)} %dynamic-update-slice), channel_id=1, replica_groups=mesh['dp'=32] {'dp'}, use_global_device_ids=true, to_apply=%add.1 | all-reduce | flops 14336 | bytes 57344
  96.0 0.6 slice.102
  96.8 0.6 copy.39.bqkv
  97.5 0.7 maximum_maximum_fusion.bias
  98.1 81.8 %all-reduce.6.cloned.1.call-done = f32[32,6144]{1,0:T(8,128)} async-done(((f32[32,6144]{1,0:T(8,128)}), f32[32,6144]{1,0:T(8,128)}) %all-reduce.6.cloned.1.call-update) | async-done | bytes 786448
  179.9 1.0 fusion.10
  181.0 0.6 concatenate.10.mod
  181.6 70.8 %all-gather.7.cloned.1.call-done.w_h = bf16[4,1024,768]{2,1,0:T(8,128)(2,1)} async-done(((bf16[4,32,768]{2,1,0:T(8,128)(2,1)}), bf16[4,1024,768]{2,1,0:T(8,128)(2,1)}) %all-gather.7.cloned.1.call-update) | async-done | bytes 6291472 | tf_op jit(solution)/shard_map/all_gather | solution.py:273
  252.3 43.2 %ka1024.1 = (bf16[4,1024,768]{2,1,0:T(8,128)(2,1)}, bf16[1024,1024]{1,0:T(8,128)(2,1)}, f32[4,4,1024]{2,1,0:T(4,128)}, bf16[1024,1024]{1,0:T(8,128)(2,1)}) custom-call(bf16[1024,1024]{1,0:T(8,128)(2,1)} %bitcast.60, f32[8,1024]{1,0:T(8,128)} %concatenate.10.mod, f32[4,1,768]{2,1,0:T(1,128)} %copy.39.bqkv, bf16[4,1024,768]{2,1,0:T(8,128)(2,1)} %all-gather.7.cloned.1.call-done.w_h), custom_call_target="tpu_custom_call" | custom-call | tf_op jit(solution)/shard_map/ka1024/pallas_call | solution.py:180
  295.5 15.6 %all-gather.9.cloned.1.call-done.wout_h = bf16[1024,1024]{1,0:T(8,128)(2,1)} async-done(((bf16[32,1024]{1,0:T(8,128)(2,1)}), bf16[1024,1024]{1,0:T(8,128)(2,1)}) %all-gather.9.cloned.1.call-update) | async-done | bytes 2097168 | tf_op jit(solution)/shard_map/all_gather | solution.py:274
  311.2 80.5 %all-gather.11.cloned.1.call-done.wup_h = bf16[8,1024,512]{2,1,0:T(8,128)(2,1)} async-done(((bf16[8,32,512]{2,1,0:T(8,128)(2,1)}), bf16[8,1024,512]{2,1,0:T(8,128)(2,1)}) %all-gather.11.cloned.1.call-update) | async-done | bytes 8388624 | tf_op jit(solution)/shard_map/all_gather | solution.py:275
  391.6 80.1 %all-gather.13.cloned.1.call-done.wdn_h = bf16[8,1024,512]{2,1,0:T(8,128)(2,1)} async-done(((bf16[8,32,512]{2,1,0:T(8,128)(2,1)}), bf16[8,1024,512]{2,1,0:T(8,128)(2,1)}) %all-gather.13.cloned.1.call-update) | async-done | bytes 8388624 | tf_op jit(solution)/shard_map/all_gather | solution.py:276
  471.7 95.3 %kb512.1 = (bf16[1024,1024]{1,0:T(8,128)(2,1)}, f32[1024,1024]{1,0:T(8,128)}, bf16[4,1024,256]{2,1,0:T(8,128)(2,1)}, f32[8,2,1024,512]{3,2,1,0:T(8,128)}, f32[10...) custom-call(bf16[1024,1024]{1,0:T(8,128)(2,1)} %bitcast.61, ...), custom_call_target="tpu_custom_call" | custom-call | tf_op jit(solution)/shard_map/kb512/pallas_call | solution.py:137
  567.1 76.3 %kc1024.1 = (f32[1024,1024]{1,0:T(8,128)}, f32[4,1024,768]{2,1,0:T(8,128)}, f32[8,1024]{1,0:T(8,128)}, f32[4,1,768]{2,1,0:T(1,128)}) custom-call(bf16[1024,1024]{1,0:T(8,128)(2,1)} %bitcast.62, f32[8,1024]{1,0:T(8,128)} %concatenate.10.mod, bf16[4,1024,768]{2,1,0:T(8,128)(2,1)} %get-tuple-element.29.qkv, bf16[4,1024,256]{2,1,0:T(8,128)(2,1)} %get-tuple-element.30.dat, ...), custom_call_target="tpu_custom_call" | custom-call | tf_op jit(solution)/shard_map/kc1024/pallas_call | solution.py:242
  643.5 0.7 reduce-scatter.8.cloned.1.call-update
  644.3 0.7 reduce-scatter.6.cloned.1.call-update
  645.2 41.4 %all-gather.1 = bf16[32,1,6144]{2,1,0:T(2,128)(2,1)S(1)} all-gather(bf16[1,1,6144]{2,1,0:T(2,128)(2,1)S(1)} %reshape.122), channel_id=1, replica_groups=mesh['dp'=32] {'dp'}, dimensions={0}, use_global_device_ids=true | all-gather | bytes 405504 | tf_op jit(solution)/shard_map/all_gather | solution.py:293
  686.5 1.0 fusion.3
  687.5 2.5 all-to-all-start
  690.1 0.8 fusion.16
  691.0 44.7 %all-reduce.3 = f32[14336]{0:T(1024)S(1)} all-reduce(f32[14336]{0:T(1024)S(1)} %constant_dynamic-update-slice_fusion), channel_id=6, replica_groups=mesh['dp'=32] {'dp'}, use_global_device_ids=true, to_apply=%region_4.5.clone | all-reduce | flops 14336 | bytes 114688
  735.6 1.3 fusion.1
  736.9 0.7 multiply_subtract_fusion.1
  737.6 0.5 broadcast.25
  738.1 0.7 reduce.7
  738.8 0.1 all_to_all.14
  738.9 0.6 multiply_multiply_fusion.1
  739.5 59.0 %reduce-scatter.4.cloned.1.call-done = f32[4,32,768]{2,1,0:T(8,128)} async-done(((f32[4,1024,768]{2,1,0:T(8,128)}), f32[4,32,768]{2,1,0:T(8,128)}) %reduce-scatter.4.cloned.1.call-update) | async-done | bytes 393232 | tf_op jit(solution)/shard_map/reduce_scatter | solution.py:289
  798.5 1.2 reshape.113
  799.7 0.3 copy.43
  800.0 0.9 reshape.114
  800.9 353.4 %reduce-scatter.8.cloned.1.call-done = f32[8,2,32,512]{3,2,1,0:T(8,128)} async-done(((f32[8,2,1024,512]{3,2,1,0:T(8,128)}), f32[8,2,32,512]{3,2,1,0:T(8,128)}) %reduce-scatter.8.cloned.1.call-update) | async-done | bytes 1048592 | tf_op jit(solution)/shard_map/reduce_scatter | solution.py:287
  1154.3 1.8 copy.44
  1156.1 0.6 copy.50
  1156.7 148.4 %reduce-scatter.6.cloned.1.call-done = f32[32,1024]{1,0:T(8,128)} async-done(((f32[1024,1024]{1,0:T(8,128)}), f32[32,1024]{1,0:T(8,128)}) %reduce-scatter.6.cloned.1.call-update) | async-done | bytes 131088 | tf_op jit(solution)/shard_map/reduce_scatter | solution.py:288
  1305.1 5.7 multiply_subtract_fusion
  (61 shorter events, 0.9 us)
Async XLA Ops:
  7.2 172.8 %all-reduce.6.cloned.1.call-start = ((), (), s32[]{:S(2)}) async-start(), calls=%async_computation.11 | async-start | bytes 1572864
  54.6 3.7 copy-start.6
  54.6 197.8 %all-gather.7.cloned.1.call-start = ((), (), s32[]{:S(2)}) async-start(), calls=%async_computation.4 | async-start | bytes 6488064 | tf_op jit(solution)/shard_map/all_gather | solution.py:273
  55.8 255.3 %all-gather.9.cloned.1.call-start = ((), (), s32[]{:S(2)}) async-start(), calls=%async_computation.5 | async-start | bytes 2162688 | tf_op jit(solution)/shard_map/all_gather | solution.py:274
  56.5 335.1 %all-gather.11.cloned.1.call-start = ((), (), s32[]{:S(2)}) async-start(), calls=%async_computation.6 | async-start | bytes 8650752 | tf_op jit(solution)/shard_map/all_gather | solution.py:275
  57.4 414.4 %all-gather.13.cloned.1.call-start = ((), (), s32[]{:S(2)}) async-start(), calls=%async_computation.7 | async-start | bytes 8650752 | tf_op jit(solution)/shard_map/all_gather | solution.py:276
  58.2 740.3 %reduce-scatter.4.cloned.1.call-start = ((), (), s32[]{:S(2)}) async-start(), calls=%async_computation.8 | async-start | bytes 12976128 | tf_op jit(solution)/shard_map/reduce_scatter | solution.py:289
  643.4 510.8 %reduce-scatter.8.cloned.1.call-start = ((), (), s32[]{:S(2)}) async-start(), calls=%async_computation.10 | async-start | bytes 34603008 | tf_op jit(solution)/shard_map/reduce_scatter | solution.py:287
  644.2 0.8 copy-start.5
  644.2 0.9 copy-start.1
  644.2 0.9 copy-start.2
  644.2 660.8 %reduce-scatter.6.cloned.1.call-start = ((), (), s32[]{:S(2)}) async-start(), calls=%async_computation.9 | async-start | bytes 4325376 | tf_op jit(solution)/shard_map/reduce_scatter | solution.py:288
  644.3 46.6 %copy-start.3 = (f32[8,1,512]{2,1,0:T(1,128)S(1)}, f32[8,1,512]{2,1,0:T(1,128)}, u32[]{:S(2)}) copy-start(f32[8,1,512]{2,1,0:T(1,128)} %get-tuple-element.42) | copy-start | bytes 49156
  645.0 91.9 %copy-start.7 = (f32[448]{0:T(512)S(1)}, f32[448]{0:T(512)}, u32[]{:S(2)}) copy-start(f32[448]{0:T(512)} %param.16) | copy-start | bytes 5380
  645.0 91.9 %copy-start.8 = (f32[448]{0:T(512)S(1)}, f32[448]{0:T(512)}, u32[]{:S(2)}) copy-start(f32[448]{0:T(512)} %param.17) | copy-start | bytes 5380
  645.0 93.9 %copy-start.4 = (f32[1,1024]{1,0:T(1,128)S(1)}, f32[1,1024]{1,0:T(1,128)}, u32[]{:S(2)}) copy-start(f32[1,1024]{1,0:T(1,128)} %param.10) | copy-start | bytes 12292
  687.5 50.1 %all-to-all-start = ((f32[32,1,32]{2,1,0:T(1,128)}), f32[32,1,32]{2,1,0:T(1,128)S(1)}, u32[]{:S(2)}, u32[]{:S(2)}) async-start(f32[32,1,32]{2,1,0:T(1,128)} %bitcast.16), calls=%async_computation | async-start | bytes 32768 | tf_op jit(solution)/shard_map/all_to_all | solution.py:296
  799.9 505.1 %copy-start = (f32[32,18432]{1,0:T(8,128)S(1)}, f32[32,18432]{1,0:T(8,128)}, u32[]{:S(2)}) copy-start(f32[32,18432]{1,0:T(8,128)} %param.12) | copy-start | bytes 7077892
Sparse Core Ops, SparseCore 0:
  54.7 125.2 all-reduce.5
  183.7 68.5 all-gather.6
  256.2 54.9 all-gather.8
  314.9 76.6 all-gather.10
  395.4 76.3 all-gather.12
  643.6 154.8 reduce-scatter.3
  800.8 353.4 reduce-scatter.7
  1156.5 148.4 reduce-scatter.5

commit v2 on v1

--- a/solution.py
+++ b/solution.py
@@ -27,6 +27,260 @@
 V = pl.BlockSpec(memory_space=pltpu.VMEM)
 A = pl.BlockSpec(memory_space=pl.ANY)
 sd = jax.ShapeDtypeStruct
+MESH = pl.DeviceIdType.MESH
+
+
+def mesh_signal(sem, dev):
+    pl.semaphore_signal(sem, inc=1, device_id=(dev,), device_id_type=MESH)
+
+
+def remote(src, dst, send, recv, dev):
+    return pltpu.make_async_remote_copy(src_ref=src, dst_ref=dst, send_sem=send, recv_sem=recv, device_id=(dev,), device_id_type=MESH)
+
+
+def greet_all(n, me):
+    barrier = pltpu.get_barrier_semaphore()
+
+    def go(k, _):
+        mesh_signal(barrier, lax.rem(me + k, n))
+        return 0
+
+    lax.fori_loop(1, n, go, 0)
+    pl.semaphore_wait(barrier, n - 1)
+
+
+def each_peer(n, me, f):
+    def go(k, _):
+        f(k, lax.rem(me + k, n), lax.rem(me + n - k, n))
+        return 0
+
+    lax.fori_loop(1, n, go, 0)
+
+
+def first_kernel(n, rows, small, ada, mod, gat, wz, part, rec, s0, r0, s1, r1):
+    me = lax.axis_index("dp")
+    greet_all(n, me)
+    each_peer(n, me, lambda k, to, fr: remote(small, gat.at[me], s0.at[k], r0.at[k], to).start())
+    gat[pl.ds(me, 1)] = small[...].reshape(1, 16, 128)
+    wz[...] = jnp.zeros_like(wz)
+    per = 128 // rows
+    wz[pl.ds(pl.multiple_of(lax.rem(me, per) * rows, rows), rows), :] = ada[...]
+    each_peer(n, me, lambda k, to, fr: remote(small, gat.at[fr], s0.at[k], r0.at[k], to).wait())
+    cond = gat[:, pl.ds(me // per, 1), :].reshape(n, 128).astype(bf)
+    for c in range(12):
+        cols = slice(c * 512, (c + 1) * 512)
+        part[:, :, cols] = dot(cond, wz[:, cols]).reshape(n, 1, 512)
+    each_peer(n, me, lambda k, to, fr: remote(part.at[to], rec.at[me], s1.at[k], r1.at[k], to).start())
+    rec[pl.ds(me, 1)] = part[pl.ds(me, 1)]
+    each_peer(n, me, lambda k, to, fr: remote(part.at[to], rec.at[fr], s1.at[k], r1.at[k], to).wait())
+    for c in range(12):
+        cols = slice(c * 512, (c + 1) * 512)
+        mod[:, cols] = jnp.sum(rec[:, :, cols], axis=0)
+
+
+def first(n, rows, small, ada):
+    return pl.pallas_call(
+        functools.partial(first_kernel, n, rows),
+        out_shape=(sd((1, 6 * D), f32), sd((n, 16, 128), f32)),
+        in_specs=[V, V],
+        out_specs=[V, V],
+        scratch_shapes=[pltpu.VMEM((128, 6 * D), bf), pltpu.VMEM((n, 1, 6 * D), f32), pltpu.VMEM((n, 1, 6 * D), f32)] + [pltpu.SemaphoreType.DMA((n,))] * 4,
+        compiler_params=pltpu.CompilerParams(collective_id=0, has_side_effects=True, vmem_limit_bytes=40 * 2**20),
+        name="first",
+    )(small, ada)
+
+
+def last_kernel(n, brow, dm, bsum, dall, rec, s0, r0, s1, r1):
+    me = lax.axis_index("dp")
+    greet_all(n, me)
+    each_peer(n, me, lambda k, to, fr: remote(dm, dall.at[me], s0.at[k], r0.at[k], to).start())
+    each_peer(n, me, lambda k, to, fr: remote(brow.at[to], rec.at[me], s1.at[k], r1.at[k], to).start())
+    dall[pl.ds(me, 1)] = dm[...].reshape(1, 48, 128)
+    rec[pl.ds(me, 1)] = brow[pl.ds(me, 1)]
+    each_peer(n, me, lambda k, to, fr: remote(dm, dall.at[fr], s0.at[k], r0.at[k], to).wait())
+    each_peer(n, me, lambda k, to, fr: remote(brow.at[to], rec.at[fr], s1.at[k], r1.at[k], to).wait())
+    bsum[...] = jnp.sum(rec[...], axis=0)
+
+
+def last(n, brow, dm):
+    return pl.pallas_call(
+        functools.partial(last_kernel, n),
+        out_shape=(sd((8, 128), f32), sd((n, 48, 128), bf)),
+        in_specs=[V, V],
+        out_specs=[V, V],
+        scratch_shapes=[pltpu.VMEM((n, 8, 128), f32)] + [pltpu.SemaphoreType.DMA((n,))] * 4,
+        compiler_params=pltpu.CompilerParams(collective_id=1, has_side_effects=True),
+        name="last",
+    )(brow, dm)
+
+
+def swap_kernel(n, cp, out, s0, r0):
+    me = lax.axis_index("dp")
+    greet_all(n, me)
+    each_peer(n, me, lambda k, to, fr: remote(cp.at[to], out.at[me], s0.at[k], r0.at[k], to).start())
+    out[pl.ds(me, 1)] = cp[pl.ds(me, 1)]
+    each_peer(n, me, lambda k, to, fr: remote(cp.at[to], out.at[fr], s0.at[k], r0.at[k], to).wait())
+
+
+def swap(n, cp):
+    return pl.pallas_call(
+        functools.partial(swap_kernel, n),
+        out_shape=sd(cp.shape, f32),
+        in_specs=[V],
+        out_specs=V,
+        scratch_shapes=[pltpu.SemaphoreType.DMA((n,))] * 2,
+        compiler_params=pltpu.CompilerParams(collective_id=2, has_side_effects=True),
+        name="swap",
+    )(cp)
+
+
+class Place:
+    def __init__(self):
+        me = lax.axis_index("dp")
+        self.me = me
+        self.z = me // 8
+        self.y = lax.rem(me // 4, 2)
+        self.x = lax.rem(me // 2, 2)
+        self.c = lax.rem(me, 2)
+        self.to_c = me + 1 - 2 * self.c
+        self.to_x = me + 2 - 4 * self.x
+        self.to_y = me + 4 - 8 * self.y
+
+    def to_z(self, k):
+        return lax.rem(self.z + k, 4) * 8 + lax.rem(self.me, 8)
+
+    def greet(self):
+        barrier = pltpu.get_barrier_semaphore()
+        for k in (1, 2, 3):
+            mesh_signal(barrier, self.to_z(k))
+        for dev in (self.to_c, self.to_x, self.to_y):
+            mesh_signal(barrier, dev)
+        pl.semaphore_wait(barrier, 6)
+
+
+class Gather:
+    def __init__(self, at, src, buf, local, send, recv, count):
+        self.at, self.src, self.buf, self.local, self.send, self.recv, self.count = at, src, buf, local, send, recv, count
+
+    def step_refs(self, i, step, c):
+        at, b = self.at, self.buf.at[i]
+        y, x = at.y, at.x
+        lo, hi = pl.ds(0, 16), pl.ds(16, 16)
+        if step == 1:
+            return [b.at[:, y, x, c]]
+        if step == 2:
+            return [b.at[:, y, 1 - x, c, lo], b.at[:, 1 - y, x, c, hi]]
+        return [b.at[:, 1 - y, :, c, lo], b.at[:, :, 1 - x, c, hi]]
+
+    def z_copy(self, i, k):
+        at = self.at
+        return remote(self.src.at[i], self.buf.at[i, at.z, at.y, at.x, at.c], self.send.at[i, k - 1], self.recv.at[i, k - 1], at.to_z(k))
+
+    def z_landed(self, i, k):
+        at = self.at
+        zz = lax.rem(at.z + 4 - k, 4)
+        return remote(self.src.at[i], self.buf.at[i, zz, at.y, at.x, at.c], self.send.at[i, k - 1], self.recv.at[i, k - 1], at.to_z(k))
+
+    def own(self, i):
+        at = self.at
+        return pltpu.make_async_copy(self.src.at[i], self.buf.at[i, at.z, at.y, at.x, at.c], self.local.at[i])
+
+    def xy_copies(self, i, step):
+        at, b = self.at, self.buf.at[i]
+        y, x, c = at.y, at.x, at.c
+        lo, hi = pl.ds(0, 16), pl.ds(16, 16)
+        if step == 2:
+            a, d = b.at[:, y, x, c, lo], b.at[:, y, x, c, hi]
+            return [
+                remote(a, a, self.send.at[i, 3], self.recv.at[i, 3], at.to_x),
+                remote(d, d, self.send.at[i, 4], self.recv.at[i, 4], at.to_y),
+            ]
+        a, d = b.at[:, y, :, c, lo], b.at[:, :, x, c, hi]
+        return [
+            remote(a, a, self.send.at[i, 5], self.recv.at[i, 5], at.to_y),
+            remote(d, d, self.send.at[i, 6], self.recv.at[i, 6], at.to_x),
+        ]
+
+    def xy_landed(self, i, step):
+        at, b = self.at, self.buf.at[i]
+        refs = self.step_refs(i, step, at.c)
+        base = 3 if step == 2 else 5
+        return [remote(r, r, self.send.at[i, base + q], self.recv.at[i, base + q], at.to_x) for q, r in enumerate(refs)]
+
+    def core_copies(self, i, step):
+        at = self.at
+        base = {1: 7, 2: 8, 3: 10}[step]
+        return [remote(r, r, self.send.at[i, base + q], self.recv.at[i, base + q], at.to_c) for q, r in enumerate(self.step_refs(i, step, at.c))]
+
+    def core_landed(self, i, step):
+        at = self.at
+        base = {1: 7, 2: 8, 3: 10}[step]
+        return [remote(r, r, self.send.at[i, base + q], self.recv.at[i, base + q], at.to_c) for q, r in enumerate(self.step_refs(i, step, 1 - at.c))]
+
+    def start(self):
+        def go(i, _):
+            self.own(i).start()
+            return 0
+
+        lax.fori_loop(0, self.count, go, 0)
+
+    def tick(self, t):
+        def when(i, f):
+            @pl.when((i >= 0) & (i < self.count))
+            def _():
+                f()
+
+        def one():
+            for k in (1, 2, 3):
+                self.z_copy(t, k).start()
+
+        def two():
+            i = t - 1
+            for k in (1, 2, 3):
+                self.z_landed(i, k).wait_recv()
+            self.own(i).wait()
+            for cp in self.xy_copies(i, 2) + self.core_copies(i, 1):
+                cp.start()
+
+        def three():
+            i = t - 2
+            for cp in self.xy_landed(i, 2):
+                cp.wait_recv()
+            for cp in self.xy_copies(i, 3) + self.core_copies(i, 2):
+                cp.start()
+
+        def four():
+            i = t - 3
+            for cp in self.xy_landed(i, 3):
+                cp.wait_recv()
+            for cp in self.core_copies(i, 3):
+                cp.start()
+
+        def five():
+            i = t - 4
+            for step in (1, 2, 3):
+                for cp in self.core_landed(i, step):
+                    cp.wait_recv()
+
+        when(t - 3, four)
+        when(t - 2, three)
+        when(t - 1, two)
+        when(t, one)
+        when(t - 4, five)
+
+    def finish(self):
+        def go(i, _):
+            for k in (1, 2, 3):
+                self.z_copy(i, k).wait_send()
+            for step in (2, 3):
+                for cp in self.xy_copies(i, step):
+                    cp.wait_send()
+            for step in (1, 2, 3):
+                for cp in self.core_copies(i, step):
+                    cp.wait_send()
+            return 0
+
+        lax.fori_loop(0, self.count, go, 0)
 
 
 def dot(a,b,dn=None):
@@ -51,17 +305,17 @@
         f(pl.ds(pl.multiple_of(i*R,R),R)); return 0
     lax.fori_loop(0,n//R,body,0)
 
-def kb_kernel(R, tok, gout, attnT, mod, bias, bup, wout_h, wup_h, wdn_h,
+def kb_kernel(R, tok, gout, attnT, mod, bias, bup, wall,
       bo_ref, dx1_ref, dat_ref, dw_h, dwout_ref, dmod_ref, db_ref, dbup_ref,
       h2, h2T, dzb, dzT, z, dh2, o_s, wout, wbuf, act, du, dwst, wsem, osem, wosem):
-    pltpu.make_async_copy(wout_h, wout, wosem).start()
+    def co(g): return pltpu.make_async_copy(wall.at[g, :, 768:1024], wout.at[:, g*256:(g+1)*256], wosem.at[g])
+    for g in range(4): co(g).start()
     def fetch(j, slot):
-        pltpu.make_async_copy(wup_h.at[j], wbuf.at[slot,0], wsem.at[slot,0]).start()
-        pltpu.make_async_copy(wdn_h.at[j], wbuf.at[slot,1], wsem.at[slot,1]).start()
+        pltpu.make_async_copy(wall.at[4 + j], wbuf.at[slot], wsem.at[slot]).start()
     fetch(0,0)
     shift1=mod[0:1];scale1=mod[1:2];gate1=mod[2:3];shift2=mod[3:4];scale2=mod[4:5];gate2=mod[5:6]
     db_ref[...]=jnp.zeros_like(db_ref); dmod_ref[...]=jnp.zeros_like(dmod_ref)
-    pltpu.make_async_copy(wout_h, wout, wosem).wait()
+    for g in range(4): co(g).wait()
     def pre(r):
         o=dot(attnT[:,r],wout[...],TN)+bias[2:3]
         o_s[r,:]=o
@@ -81,19 +335,18 @@
         slot=lax.rem(j,2)
         @pl.when(j+1<NJ)
         def _(): fetch(j+1,1-slot)
-        pltpu.make_async_copy(wup_h.at[j], wbuf.at[slot,0], wsem.at[slot,0]).wait()
-        pltpu.make_async_copy(wdn_h.at[j], wbuf.at[slot,1], wsem.at[slot,1]).wait()
+        pltpu.make_async_copy(wall.at[4 + j], wbuf.at[slot], wsem.at[slot]).wait()
         dbup_ref[j]=jnp.zeros((1,CH),f32)
         def row(r):
-            u=dot(h2[r,:],wbuf[slot,0])+bup[j]
+            u=dot(h2[r,:],wbuf[slot,:,:CH])+bup[j]
             a,sl=gelu_pair(u)
             ab=a.astype(bf); act[r,:]=ab
-            da=dot(dzb[r,:],wbuf[slot,1])
+            da=dot(dzb[r,:],wbuf[slot,:,CH:])
             d=da*sl
             dbup_ref[j]+=jnp.sum(d,axis=0,keepdims=True)
             db_=d.astype(bf); du[r,:]=db_
-            z[r,:]+=dot(ab,wbuf[slot,1],NT)
-            dh2[r,:]+=dot(db_,wbuf[slot,0],NT)
+            z[r,:]+=dot(ab,wbuf[slot,:,CH:],NT)
+            dh2[r,:]+=dot(db_,wbuf[slot,:,:CH],NT)
         rows_loop(S,R,row)
         @pl.when(j>=2)
         def _():
@@ -136,55 +389,109 @@
     sd=jax.ShapeDtypeStruct
     return pl.pallas_call(functools.partial(kb_kernel,R),
       out_shape=(sd((S,D),bf),sd((S,D),f32),sd((4,S,256),bf),sd((NJ,2,D,CH),f32),sd((D,D),f32),sd((8,D),f32),sd((8,D),f32),sd((NJ,1,CH),f32)),
-      in_specs=[V]*6+[A]*3, out_specs=[V,V,V,A,V,V,V,V],
-      scratch_shapes=[pltpu.VMEM((S,D),bf)]*4+[pltpu.VMEM((S,D),f32)]*3+[pltpu.VMEM((D,D),bf),pltpu.VMEM((2,2,D,CH),bf),pltpu.VMEM((S,CH),bf),pltpu.VMEM((S,CH),bf),
-         pltpu.VMEM((2,2,D,CH),f32),pltpu.SemaphoreType.DMA((2,2)),pltpu.SemaphoreType.DMA((2,)),pltpu.SemaphoreType.DMA],
+      in_specs=[V]*6+[A], out_specs=[V,V,V,A,V,V,V,V],
+      scratch_shapes=[pltpu.VMEM((S,D),bf)]*4+[pltpu.VMEM((S,D),f32)]*3+[pltpu.VMEM((D,D),bf),pltpu.VMEM((2,D,2*CH),bf),pltpu.VMEM((S,CH),bf),pltpu.VMEM((S,CH),bf),
+         pltpu.VMEM((2,2,D,CH),f32),pltpu.SemaphoreType.DMA((2,)),pltpu.SemaphoreType.DMA((2,)),pltpu.SemaphoreType.DMA((4,))],
       compiler_params=pltpu.CompilerParams(vmem_limit_bytes=62*2**20), name=f"kb{R}")(*a)
 
-def ka_kernel(QB, tok, mod, bqkv, w_h, qkv, attnT, lse, h1T, h1, wbuf, wsem):
-    c=LOG2E/8.0
-    def cp(g,slot): return pltpu.make_async_copy(w_h.at[g], wbuf.at[slot], wsem.at[slot])
-    cp(0,0).start()
-    shift1=mod[0:1]; scale1=mod[1:2]
+def ka_kernel(comm, tok, mod, bqkv, w_in, qkv, attnT, lse, h1T, *rest):
+    c = LOG2E / 8.0
+    if comm:
+        wall, h1, wbuf, wsem, local, send, recv = rest
+        at = Place()
+        at.greet()
+        gather = Gather(at, w_in, wall, local, send, recv, 12)
+        gather.start()
+        gather.tick(0)
+    else:
+        wall = w_in
+        h1, wbuf, wsem = rest
+
+    def cp(g, slot):
+        return pltpu.make_async_copy(wall.at[g, :, :, :, :, :, 0:768], wbuf.at[slot], wsem.at[slot])
+
+    shift1 = mod[0:1]
+    scale1 = mod[1:2]
+
     def ln(r):
-        xh,_=nrm(tok[r,:].astype(f32))
-        h1[r,:]=(xh*(1.0+scale1)+shift1).astype(bf)
-    rows_loop(S,128,ln)
+        xh, _ = nrm(tok[r, :].astype(f32))
+        h1[r, :] = (xh * (1.0 + scale1) + shift1).astype(bf)
+
+    rows_loop(S, 128, ln)
+    if comm:
+        gather.tick(1)
     for i in range(4):
-        r=slice(i*256,(i+1)*256); h1T[:,r]=h1[r,:].T
-    def group(g,_):
-        slot=lax.rem(g,2)
-        @pl.when(g<3)
-        def _(): cp(g+1,1-slot).start()
-        cp(g,slot).wait()
+        r = slice(i * 256, (i + 1) * 256)
+        h1T[:, r] = h1[r, :].T
+    if comm:
+        for t in (2, 3, 4):
+            gather.tick(t)
+    cp(0, 0).start()
+
+    def group(g, _):
+        slot = lax.rem(g, 2)
+        if comm:
+            gather.tick(5 + 2 * g)
+
+        @pl.when(g < 3)
+        def _():
+            cp(g + 1, 1 - slot).start()
+
+        cp(g, slot).wait()
+
         def proj(r):
-            qkv[g,r,:]=(dot(h1[r,:],wbuf[slot])+bqkv[g]).astype(bf)
-        rows_loop(S,256,proj)
+            qkv[g, r, :] = (dot(h1[r, :], wbuf[slot].reshape(D, 768)) + bqkv[g]).astype(bf)
+
+        rows_loop(S, 256, proj)
         for p in range(2):
-            kp=qkv[g,:,256+p*128:256+(p+1)*128]; vp=qkv[g,:,512+p*128:512+(p+1)*128]
-            ks=[lane_half(kp,h) for h in range(2)]; vT=vp.T
-            for i in range(S//QB):
-                q=qkv[g,i*QB:(i+1)*QB,p*128:(p+1)*128]
-                for h in range(2):
-                    s=dot(ks[h],q,NT)
-                    m=jnp.max(s,axis=0,keepdims=True)
-                    e=jnp.exp2((s-m)*c)
-                    l=jnp.sum(e,axis=0,keepdims=True)
-                    pr=(e*(1.0/l)).astype(bf)
-                    o=dot(vT[h*64:(h+1)*64],pr)
-                    lse[g,p*2+h:p*2+h+1,i*QB:(i+1)*QB]=m*0.125+jnp.log(l)
-                    attnT[pl.ds(pl.multiple_of(g*256+(p*128+h*64),64),64),i*QB:(i+1)*QB]=o.astype(bf)
+            if comm and p == 1:
+                gather.tick(6 + 2 * g)
+            kp = qkv[g, :, 256 + p * 128 : 256 + (p + 1) * 128]
+            vp = qkv[g, :, 512 + p * 128 : 512 + (p + 1) * 128]
+            q = qkv[g, :, p * 128 : (p + 1) * 128]
+            vT = vp.T
+            for h in range(2):
+                s = dot(lane_half(kp, h), q, NT)
+                m = jnp.max(s, axis=0, keepdims=True)
+                e = jnp.exp2((s - m) * c)
+                l = jnp.sum(e, axis=0, keepdims=True)
+                pr = (e * (1.0 / l)).astype(bf)
+                o = dot(vT[h * 64 : (h + 1) * 64], pr)
+                lse[g, p * 2 + h : p * 2 + h + 1, :] = m * 0.125 + jnp.log(l)
+                attnT[pl.ds(pl.multiple_of(g * 256 + (p * 128 + h * 64), 64), 64), :] = o.astype(bf)
         return 0
-    lax.fori_loop(0,4,group,0)
-def ka(QB,*a):
-    return pl.pallas_call(functools.partial(ka_kernel,QB),
-      out_shape=(sd((4,S,768),bf),sd((D,S),bf),sd((4,4,S),f32),sd((D,S),bf)),
-      in_specs=[V,V,V,A], out_specs=[V]*4,
-      scratch_shapes=[pltpu.VMEM((S,D),bf),pltpu.VMEM((2,D,768),bf),pltpu.SemaphoreType.DMA((2,))],
-      compiler_params=pltpu.CompilerParams(vmem_limit_bytes=60*2**20), name=f"ka{QB}")(*a)
+
+    lax.fori_loop(0, 4, group, 0)
+    if comm:
+        for t in (13, 14, 15):
+            gather.tick(t)
+        gather.finish()
+
+
+def ka(comm, *a):
+    out = (sd((4, S, 768), bf), sd((D, S), bf), sd((4, 4, S), f32), sd((D, S), bf))
+    scratch = [pltpu.VMEM((S, D), bf), pltpu.VMEM((2, 4, 2, 2, 2, 32, 768), bf), pltpu.SemaphoreType.DMA((2,))]
+    params = dict(vmem_limit_bytes=60 * 2**20)
+    specs = [V] * 4
+    if comm:
+        out += (sd((12, 4, 2, 2, 2, 32, 1024), bf),)
+        specs += [A]
+        scratch += [pltpu.SemaphoreType.DMA((12,)), pltpu.SemaphoreType.DMA((12, 12)), pltpu.SemaphoreType.DMA((12, 12))]
+        params.update(collective_id=3, has_side_effects=True)
+    return pl.pallas_call(
+        functools.partial(ka_kernel, comm),
+        out_shape=out,
+        in_specs=[V, V, V, A],
+        out_specs=specs,
+        scratch_shapes=scratch,
+        compiler_params=pltpu.CompilerParams(**params),
+        name="attention_forward",
+    )(*a)
+
+
 def kc_kernel(QB, tok, mod, qkv, dat, lse, dx1, h1T, w_h, ig, dw_h, dmod, dbq, dqkv, dk_s, dv_s, dqT_s, dh1, wbuf, dwst, wsem, osem):
     c=LOG2E/8.0
-    def cp(g,slot): return pltpu.make_async_copy(w_h.at[g], wbuf.at[slot], wsem.at[slot])
+    def cp(g,slot): return pltpu.make_async_copy(w_h.at[g, :, 0:768], wbuf.at[slot], wsem.at[slot])
     def co(g,slot): return pltpu.make_async_copy(dwst.at[slot], dw_h.at[g], osem.at[slot])
     cp(0,0).start()
     dh1[...]=jnp.zeros_like(dh1); dmod[...]=jnp.zeros_like(dmod); dbq[...]=jnp.zeros_like(dbq)
@@ -258,42 +565,62 @@
 def on_device(n, block_in, condition, out_grad, weights, biases, first_moment, second_moment, bias_first, bias_second):
     me = lax.axis_index("dp")
     rows = D // n
+    chips = n == 32
     wb = weights.astype(bf)
-    qkv_l = wb[:, : 3 * D].reshape(rows, 3, 4, 256).transpose(2, 0, 1, 3).reshape(4, rows, 768)
-    up_l = wb[:, 4 * D : 4 * D + FF].reshape(rows, NJ, CH).transpose(1, 0, 2)
-    dn_l = wb[:, 4 * D + FF : 4 * D + 2 * FF].reshape(rows, NJ, CH).transpose(1, 0, 2)
+    qkvo = wb[:, : 4 * D].reshape(rows, 4, 4, 256).transpose(2, 0, 1, 3).reshape(4, rows, 1024)
+    updn = wb[:, 4 * D : 4 * D + 2 * FF].reshape(rows, 2, NJ, CH).transpose(2, 0, 1, 3).reshape(NJ, rows, 1024)
+    mine = jnp.concatenate([qkvo, updn], axis=0)
     ada_l = wb[:, 4 * D + 2 * FF :]
-    bias_full = lax.all_gather(biases.astype(bf), "dp", axis=0, tiled=True).astype(f32)
     cond_act = jax.nn.silu(condition).astype(bf)
-    cond_all = lax.all_gather(cond_act, "dp", axis=0, tiled=True)
+    if chips:
+        small = jnp.concatenate([cond_act.astype(f32).reshape(-1), lax.reduce_precision(biases, 8, 7), jnp.zeros((576,), f32)])
+        mod, gat = first(n, rows, small.reshape(16, 128), ada_l)
+        bias_full = gat[:, 8:12].reshape(n, 512)[:, : biases.shape[0]].reshape(-1)
+        cond_all = gat[:, :8].reshape(n, D).astype(bf)
+    else:
+        bias_full = lax.all_gather(biases.astype(bf), "dp", axis=0, tiled=True).astype(f32)
+        cond_all = lax.all_gather(cond_act, "dp", axis=0, tiled=True)
     cond_cols = lax.dynamic_slice_in_dim(cond_all, me * rows, rows, 1)
-    mod_part = jnp.dot(cond_cols, ada_l, preferred_element_type=f32)
-    mod = lax.psum_scatter(mod_part, "dp", scatter_dimension=0, tiled=True) + bias_full[4 * D + FF :]
+    if not chips:
+        mod = lax.psum_scatter(jnp.dot(cond_cols, ada_l, preferred_element_type=f32), "dp", scatter_dimension=0, tiled=True)
+    mod = mod + bias_full[4 * D + FF :]
     mod = jnp.concatenate([mod.reshape(6, D), jnp.zeros((2, D), f32)], axis=0)
-    w_qkv = lax.all_gather(qkv_l, "dp", axis=1, tiled=True)
-    w_out = lax.all_gather(wb[:, 3 * D : 4 * D], "dp", axis=0, tiled=True)
-    w_up = lax.all_gather(up_l, "dp", axis=1, tiled=True)
-    w_dn = lax.all_gather(dn_l, "dp", axis=1, tiled=True)
     zrow = jnp.zeros((D,), f32)
     bqkv = jnp.stack([bias_full[:D], zrow, bias_full[D : 2 * D]]).reshape(3, 4, 256).transpose(1, 0, 2).reshape(4, 1, 768)
     brows = jnp.stack([zrow, zrow, bias_full[2 * D : 3 * D], bias_full[3 * D + FF : 4 * D + FF], zrow, zrow, zrow, zrow])
     bup = bias_full[3 * D : 3 * D + FF].reshape(NJ, 1, CH)
     tok = block_in[0]
     gout = out_grad[0]
-    qkv, attn_t, lse, h1t = ka(1024, tok, mod, bqkv, w_qkv)
-    bo, dx1, dat, dw_mlp, dw_out, dmod_b, db, db_up = kb(512, tok, gout, attn_t, mod, brows, bup, w_out, w_up, w_dn)
-    ig, dw_qkv, dmod_a, db_qkv = kc(1024, tok, mod, qkv, dat, lse, dx1, h1t, w_qkv)
+    if chips:
+        qkv, attn_t, lse, h1t, wall = ka(True, tok, mod, bqkv, mine)
+    else:
+        wall = lax.all_gather(mine, "dp", axis=1, tiled=True).reshape(12, 4, 2, 2, 2, 32, 1024)
+        qkv, attn_t, lse, h1t = ka(False, tok, mod, bqkv, wall)
+    wall = wall.reshape(12, D, 1024)
+    bo, dx1, dat, dw_mlp, dw_out, dmod_b, db, db_up = kb(512, tok, gout, attn_t, mod, brows, bup, wall)
+    ig, dw_qkv, dmod_a, db_qkv = kc(1024, tok, mod, qkv, dat, lse, dx1, h1t, wall)
     dmod = (dmod_a + dmod_b)[:6].reshape(1, 6 * D)
     g_mlp = lax.psum_scatter(dw_mlp, "dp", scatter_dimension=2, tiled=True)
     g_out = lax.psum_scatter(dw_out, "dp", scatter_dimension=0, tiled=True)
     g_qkv = lax.psum_scatter(dw_qkv, "dp", scatter_dimension=1, tiled=True)
     db_qkv = db_qkv.reshape(4, 3, 256).transpose(1, 0, 2).reshape(3, D)
     bias_row = jnp.concatenate([db_qkv[0], db_qkv[2], db[2], db_up.reshape(FF), db[3], dmod[0]])
-    bias_grad = lax.psum_scatter(bias_row, "dp", scatter_dimension=0, tiled=True)
-    dmod_all = lax.all_gather(dmod.astype(bf), "dp", axis=0, tiled=True)
+    dmod_bf = dmod.astype(bf)
+    if chips:
+        own = biases.shape[0]
+        blocks = jnp.pad(bias_row.reshape(n, own), ((0, 0), (0, 1024 - own))).reshape(n, 8, 128)
+        bias_grad, dmod_all = last(n, blocks, dmod_bf.reshape(48, 128))
+        bias_grad = bias_grad.reshape(-1)[:own]
+        dmod_all = dmod_all.reshape(n, 6 * D)
+    else:
+        bias_grad = lax.psum_scatter(bias_row, "dp", scatter_dimension=0, tiled=True)
+        dmod_all = lax.all_gather(dmod_bf, "dp", axis=0, tiled=True)
     g_ada = lax.dot_general(cond_cols, dmod_all, TN, preferred_element_type=f32)
     cond_part = lax.dot_general(dmod_all, ada_l, NT, preferred_element_type=f32)
-    cond_grad = lax.all_to_all(cond_part, "dp", split_axis=0, concat_axis=1, tiled=True)
+    if chips:
+        cond_grad = swap(n, jnp.pad(cond_part, ((0, 0), (0, 128 - rows))).reshape(n, 1, 128))[:, 0, :rows].reshape(1, D)
+    else:
+        cond_grad = lax.all_to_all(cond_part, "dp", split_axis=0, concat_axis=1, tiled=True)
     sigma = jax.nn.sigmoid(condition)
     cond_grad = cond_grad * (sigma * (1.0 + condition * (1.0 - sigma)))
     g_qkv = g_qkv.reshape(4, rows, 3, 256).transpose(1, 2, 0, 3).reshape(rows, 3 * D)

time: 1320 us -> 1040 us (0.79)
  waiting for transfers between devices: 891 us -> 619 us
  blocking collectives: 167 us -> 0 us
  Pallas kernels: 215 us -> 373 us
    all_gather x4 -> x0, waiting for transfers between devices: 247 us -> none  [the longest x1 80.5 us: on_device(): w_up = lax.all_gather(up_l, 'dp', axis=1, tiled=True)]
    pallas_call x1 -> x4, Pallas kernels: 43.2 us -> 201 us  [the longest x1 143 us: ka(): pl.pallas_call(functools.partial(ka_kernel, comm), out_shape=out, in_spec...]
    all_gather x2 -> x0, blocking collectives: 84.9 us -> none  [the longest x1 43.6 us: on_device(): cond_all = lax.all_gather(cond_act, 'dp', axis=0, tiled=True)]
    unnamed x2 -> x0, blocking collectives: 82.1 us -> none
    unnamed x9 -> x3, waiting for transfers between devices: 83.3 us -> 1.36 us
    reduce_scatter x1, waiting for transfers between devices: 59 us -> 116 us  [on_device(): g_qkv = lax.psum_scatter(dw_qkv, 'dp', scatter_dimension=1, tiled=True)]
  transfers between devices with their start and end apart: 9 -> 3, of which waited for: 8 -> 3; matrix products, arithmetic and copies ran while one was open for 1% -> 1% of each run, Pallas kernels for 3% -> 3%
where the time goes in v2:
time: 1040 us
  waiting for transfers between devices  619 us (60%)
  Pallas kernels  373 us (36%)
  between operations  14.6 us (1%)
  local copies, waits for them, and re-layouts  13.3 us (1%)
  other arithmetic  12.2 us (1%)
    reduce_scatter x1, waiting for transfers between devices, on_device(): g_mlp = lax.psum_scatter(dw_mlp, 'dp', scatter_dimension=2, tiled=True)  353 us
    reduce_scatter x1, waiting for transfers between devices, on_device(): g_out = lax.psum_scatter(dw_out, 'dp', scatter_dimension=0, tiled=True)  149 us
    pallas_call x1, Pallas kernels, ka(): pl.pallas_call(functools.partial(ka_kernel, comm), out_shape=out, in_spec...  143 us
    reduce_scatter x1, waiting for transfers between devices, on_device(): g_qkv = lax.psum_scatter(dw_qkv, 'dp', scatter_dimension=1, tiled=True)  116 us
    pallas_call x1, Pallas kernels, kb(): pl.pallas_call(functools.partial(kb_kernel, R), out_shape=(sd((S, D), bf)...  95.2 us
    pallas_call x1, Pallas kernels, kc(): pl.pallas_call(functools.partial(kc_kernel, QB), out_shape=(sd((S, D), f3...  76.8 us
    pallas_call x1, Pallas kernels, first(): pl.pallas_call(functools.partial(first_kernel, n, rows), out_shape=(sd((1...  27 us
    pallas_call x1, Pallas kernels, last(): pl.pallas_call(functools.partial(last_kernel, n), out_shape=(sd((8, 128),...  21.3 us
  transfers between devices with their start and end apart: 3, of which 3 were waited for; matrix products, arithmetic and copies ran while one was open for 1% of the time, Pallas kernels for 3%

profile of v2, /device:TPU:0, one launch (start us, length us, event | category | flops | bytes accessed | tf_op | source)
XLA Modules:
  0.0 1035.7 jit_solution(15765443722740355135)
XLA Ops:
  7.2 1.8 convert_element_type.25
  9.2 0.1 concatenate.16
  9.2 27.0 %first.1 = (f32[1,6144]{1,0:T(1,128)S(1)}, f32[32,16,128]{2,1,0:T(8,128)S(1)}) custom-call(f32[16,128]{1,0:T(8,128)S(1)} %bitcast.60, bf16[32,6144]{1,0:T(8,128)(2,1)S(1)} %slice.88.ada), custom_call_target="tpu_custom_call" | custom-call | tf_op jit(solution)/shard_map/first/pallas_call | solution.py:82
  36.3 0.1 reshape.119
  36.4 0.1 slice.78
  36.5 0.1 slice.71
  36.7 0.1 pad.22.clone
  36.8 0.1 pad.18.clone
  36.9 0.2 reshape.122
  37.0 0.1 copy.57
  37.1 0.9 reshape.123
  38.0 0.1 add_reduce_fusion
  38.1 0.6 concatenate.17.mod
  38.7 0.6 slice.97.bup
  39.3 0.1 pad_maximum_fusion.2
  39.4 0.6 copy.32.bqkv
  40.0 0.2 copy.37
  40.2 0.4 copy.56
  40.6 0.4 reshape.125
  41.0 1.9 pad_maximum_fusion.1.w_in
  42.9 0.7 maximum_maximum_fusion.bias
  43.6 142.9 %attention_forward.1 = (bf16[4,1024,768]{2,1,0:T(8,128)(2,1)}, bf16[1024,1024]{1,0:T(8,128)(2,1)}, f32[4,4,1024]{2,1,0:T(4,128)}, bf16[1024,1024]{1,0:T(8,128)(2,1)}, bf16[12,4,2,2,2,32,1024]{6,5,4,3,2,1,0:T(8,128)(2,1)}) custom-call(bf16[1024,1024]{1,0:T(8,128)(2,1)} %bitcast.63, f32[8,1024]{1,0:T(8,128)} %concatenate.17.mod, f32[4,1,768]{2,1,0:T(1,128)} %copy.32.bqkv, ...), custom_call_target="tpu_custom_call" | custom-call | tf_op jit(solution)/shard_map/attention_forward/pallas_call | solution.py:481
  186.5 95.2 %kb512.1 = (bf16[1024,1024]{1,0:T(8,128)(2,1)}, f32[1024,1024]{1,0:T(8,128)}, bf16[4,1024,256]{2,1,0:T(8,128)(2,1)}, f32[8,2,1024,512]{3,2,1,0:T(8,128)}, f32[10...) custom-call(bf16[1024,1024]{1,0:T(8,128)(2,1)} %bitcast.64, ...), custom_call_target="tpu_custom_call" | custom-call | tf_op jit(solution)/shard_map/kb512/pallas_call | solution.py:390
  281.7 76.8 %kc1024.1 = (f32[1024,1024]{1,0:T(8,128)}, f32[4,1024,768]{2,1,0:T(8,128)}, f32[8,1024]{1,0:T(8,128)}, f32[4,1,768]{2,1,0:T(1,128)}) custom-call(bf16[1024,1024]{1,0:T(8,128)(2,1)} %bitcast.65, f32[8,1024]{1,0:T(8,128)} %concatenate.17.mod, bf16[4,1024,768]{2,1,0:T(8,128)(2,1)} %get-tuple-element.37.qkv, bf16[4,1024,256]{2,1,0:T(8,128)(2,1)} %get-tuple-element.38.dat, ...), custom_call_target="tpu_custom_call" | custom-call | tf_op jit(solution)/shard_map/kc1024/pallas_call | solution.py:549
  358.6 0.7 reduce-scatter.8.cloned.1.call-update
  359.4 0.6 reduce-scatter.6.cloned.1.call-update
  360.2 0.6 convert_element_type.27.dm
  360.9 0.8 fusion.16
  361.8 0.1 reshape.129
  361.9 0.7 copy.40
  362.5 21.3 %last.1 = (f32[8,128]{1,0:T(8,128)}, bf16[32,48,128]{2,1,0:T(8,128)(2,1)}) custom-call(f32[32,8,128]{2,1,0:T(8,128)} %bitcast.78, bf16[48,128]{1,0:T(8,128)(2,1)} %convert_element_type.27.dm), custom_call_target="tpu_custom_call" | custom-call | tf_op jit(solution)/shard_map/last/pallas_call | solution.py:106
  383.8 1.3 fusion.3
  385.1 0.6 pad.10
  385.7 9.4 swap.1
  395.1 0.8 slice_reduce_fusion
  395.9 0.1 reshape_squeeze.3
  396.0 0.6 multiply_multiply_fusion.1
  396.6 1.3 multiply_subtract_fusion.1
  397.9 2.3 fusion.1
  400.2 115.9 %reduce-scatter.4.cloned.1.call-done = f32[4,32,768]{2,1,0:T(8,128)} async-done(((f32[4,1024,768]{2,1,0:T(8,128)}), f32[4,32,768]{2,1,0:T(8,128)}) %reduce-scatter.4.cloned.1.call-update) | async-done | bytes 393232 | tf_op jit(solution)/shard_map/reduce_scatter | solution.py:605
  516.1 1.2 reshape.133
  517.3 0.3 copy.34
  517.6 1.0 reshape.134
  518.5 353.4 %reduce-scatter.8.cloned.1.call-done = f32[8,2,32,512]{3,2,1,0:T(8,128)} async-done(((f32[8,2,1024,512]{3,2,1,0:T(8,128)}), f32[8,2,32,512]{3,2,1,0:T(8,128)}) %reduce-scatter.8.cloned.1.call-update) | async-done | bytes 1048592 | tf_op jit(solution)/shard_map/reduce_scatter | solution.py:603
  871.9 1.8 copy.35
  873.8 0.6 copy.42
  874.4 148.6 %reduce-scatter.6.cloned.1.call-done = f32[32,1024]{1,0:T(8,128)} async-done(((f32[1024,1024]{1,0:T(8,128)}), f32[32,1024]{1,0:T(8,128)}) %reduce-scatter.6.cloned.1.call-update) | async-done | bytes 131088 | tf_op jit(solution)/shard_map/reduce_scatter | solution.py:604
  1023.0 5.7 multiply_subtract_fusion
  (52 shorter events, 0.4 us)
Async XLA Ops:
  7.2 1.9 copy-start.6
  7.2 1.9 copy-start.4
  7.2 508.9 %reduce-scatter.4.cloned.1.call-start = ((), (), s32[]{:S(2)}) async-start(), calls=%async_computation.3 | async-start | bytes 12976128 | tf_op jit(solution)/shard_map/reduce_scatter | solution.py:605
  358.6 513.4 %reduce-scatter.8.cloned.1.call-start = ((), (), s32[]{:S(2)}) async-start(), calls=%async_computation.5 | async-start | bytes 34603008 | tf_op jit(solution)/shard_map/reduce_scatter | solution.py:603
  359.3 0.8 copy-start.5
  359.3 0.9 copy-start.1
  359.3 0.9 copy-start.2
  359.3 663.7 %reduce-scatter.6.cloned.1.call-start = ((), (), s32[]{:S(2)}) async-start(), calls=%async_computation.4 | async-start | bytes 4325376 | tf_op jit(solution)/shard_map/reduce_scatter | solution.py:604
  359.4 2.3 copy-start.3
  359.4 37.2 %copy-start.7 = (f32[448]{0:T(512)S(1)}, f32[448]{0:T(512)}, u32[]{:S(2)}) copy-start(f32[448]{0:T(512)} %param.16) | copy-start | bytes 5380
  359.4 37.2 %copy-start.8 = (f32[448]{0:T(512)S(1)}, f32[448]{0:T(512)}, u32[]{:S(2)}) copy-start(f32[448]{0:T(512)} %param.17) | copy-start | bytes 5380
  517.6 505.4 %copy-start = (f32[32,18432]{1,0:T(8,128)S(1)}, f32[32,18432]{1,0:T(8,128)}, u32[]{:S(2)}) copy-start(f32[32,18432]{1,0:T(8,128)} %param.12) | copy-start | bytes 7077892
Sparse Core Ops, SparseCore 0:
  358.7 157.3 reduce-scatter.3
  518.5 353.4 reduce-scatter.7
  874.3 148.6 reduce-scatter.5

commit v3 on v2

--- a/solution.py
+++ b/solution.py
@@ -552,6 +552,419 @@
       scratch_shapes=[pltpu.VMEM((S,768),bf),pltpu.VMEM((S,128),f32),pltpu.VMEM((S,128),f32),pltpu.VMEM((128,S),f32),pltpu.VMEM((S,D),f32),
         pltpu.VMEM((2,D,768),bf),pltpu.VMEM((2,D,768),f32),pltpu.SemaphoreType.DMA((2,)),pltpu.SemaphoreType.DMA((2,))],
       compiler_params=pltpu.CompilerParams(vmem_limit_bytes=60*2**20), name=f"kc{QB}")(*a)
+def when(cond, f):
+    @pl.when(cond)
+    def _():
+        f()
+
+
+class Pair:
+    def __init__(self, at, own, theirs, send, recv, credit, count):
+        self.at, self.own, self.theirs, self.sems, self.credit, self.count = at, own, theirs, (send, recv), credit, count
+
+    def copy(self, i):
+        slot = lax.rem(i, 2)
+        return remote(self.own.at[slot], self.theirs.at[slot], self.sems[0].at[slot], self.sems[1].at[slot], self.at.to_c)
+
+    def reuse(self, i):
+        when(i >= 2, lambda: self.copy(i).wait_send())
+
+    def start(self, i):
+        when(i >= 2, lambda: pl.semaphore_wait(self.credit, 1))
+        self.copy(i).start()
+
+    def arrived(self, i):
+        self.copy(i).wait_recv()
+
+    def free(self, i):
+        when(i + 2 < self.count, lambda: mesh_signal(self.credit, self.at.to_c))
+
+    def finish(self):
+        for i in (self.count - 2, self.count - 1):
+            self.copy(i).wait_send()
+
+
+class Scatter:
+    shapes = [
+        pltpu.VMEM((4, 2, 2, 32, 1024), f32),
+        pltpu.VMEM((2, 4, 2, 16, 1024), bf),
+        pltpu.VMEM((2, 4, 2, 16, 1024), f32),
+        pltpu.VMEM((2, 2, 4, 2, 16, 1024), bf),
+        pltpu.VMEM((2, 4, 16, 1024), bf),
+        pltpu.VMEM((2, 4, 16, 1024), f32),
+        pltpu.VMEM((2, 2, 4, 16, 1024), bf),
+        pltpu.VMEM((4, 32, 1024), bf),
+        pltpu.VMEM((32, 1024), f32),
+        pltpu.VMEM((2, 3, 32, 1024), bf),
+        pltpu.SemaphoreType.DMA((7,)),
+        pltpu.SemaphoreType.DMA((2, 7)),
+        pltpu.SemaphoreType.REGULAR((7,)),
+    ]
+
+    def __init__(self, at, refs, out, count):
+        self.at, self.out, self.count = at, out, count
+        self.acc, self.s2, self.k2, self.r2, self.s3, self.k3, self.r3, self.s4, self.k4, self.r4, self.send, self.recv, self.credit = refs
+
+    def copies(self, stage, i):
+        at = self.at
+        slot = lax.rem(i, 2)
+        if stage == 2:
+            todo = [(0, self.s2.at[0], self.r2.at[slot, 0], at.to_y), (1, self.s2.at[1], self.r2.at[slot, 1], at.to_x)]
+        elif stage == 3:
+            todo = [(2, self.s3.at[0], self.r3.at[slot, 0], at.to_x), (3, self.s3.at[1], self.r3.at[slot, 1], at.to_y)]
+        else:
+            todo = [(3 + k, self.s4.at[lax.rem(at.z + k, 4)], self.r4.at[slot, k - 1], at.to_z(k)) for k in (1, 2, 3)]
+        return [remote(src, dst, self.send.at[q], self.recv.at[slot, q], dev) for q, src, dst, dev in todo]
+
+    def sources(self, stage):
+        at = self.at
+        if stage == 2:
+            return [(0, at.to_y), (1, at.to_x)]
+        if stage == 3:
+            return [(2, at.to_x), (3, at.to_y)]
+        return [(3 + k, at.to_z(4 - k)) for k in (1, 2, 3)]
+
+    def reuse(self, stage, i):
+        def go():
+            for cp in self.copies(stage, i - 1):
+                cp.wait_send()
+
+        when(i >= 1, go)
+
+    def start(self, stage, i):
+        def go():
+            for q, _ in self.sources(stage):
+                pl.semaphore_wait(self.credit.at[q], 1)
+
+        when(i >= 2, go)
+        for cp in self.copies(stage, i):
+            cp.start()
+
+    def arrived(self, stage, i):
+        for cp in self.copies(stage, i):
+            cp.wait_recv()
+
+    def free(self, stage, i):
+        def go():
+            for q, dev in self.sources(stage):
+                mesh_signal(self.credit.at[q], dev)
+
+        when(i + 2 < self.count, go)
+
+    def two(self, i):
+        y, x = self.at.y, self.at.x
+        lo, hi = pl.ds(0, 16), pl.ds(16, 16)
+        self.reuse(2, i)
+        self.s2[0] = self.acc[:, 1 - y, :, lo, :].astype(bf)
+        self.s2[1] = self.acc[:, :, 1 - x, hi, :].astype(bf)
+        self.start(2, i)
+        self.k2[0] = self.acc[:, y, :, lo, :]
+        self.k2[1] = self.acc[:, :, x, hi, :]
+
+    def three(self, i):
+        y, x = self.at.y, self.at.x
+        slot = lax.rem(i, 2)
+        self.arrived(2, i)
+        self.reuse(3, i)
+        self.s3[0] = (self.k2[0, :, 1 - x] + self.r2[slot, 0, :, 1 - x].astype(f32)).astype(bf)
+        self.s3[1] = (self.k2[1, :, 1 - y] + self.r2[slot, 1, :, 1 - y].astype(f32)).astype(bf)
+        self.start(3, i)
+        self.k3[0] = self.k2[0, :, x] + self.r2[slot, 0, :, x].astype(f32)
+        self.k3[1] = self.k2[1, :, y] + self.r2[slot, 1, :, y].astype(f32)
+        self.free(2, i)
+
+    def four(self, i):
+        z = self.at.z
+        slot = lax.rem(i, 2)
+        self.arrived(3, i)
+        self.reuse(4, i)
+        for h in (0, 1):
+            rows = slice(16 * h, 16 * h + 16)
+            t = self.k3[h] + self.r3[slot, h].astype(f32)
+            self.s4[:, rows, :] = t.astype(bf)
+            self.k4[rows, :] = self.k3[h, z] + self.r3[slot, h, z].astype(f32)
+        self.start(4, i)
+        self.free(3, i)
+
+    def five(self, i):
+        slot = lax.rem(i, 2)
+        self.arrived(4, i)
+        t = self.k4[...]
+        for k in (0, 1, 2):
+            t = t + self.r4[slot, k].astype(f32)
+        self.out[i] = t
+        self.free(4, i)
+
+    def tick(self, t):
+        when((t >= 3) & (t - 3 < self.count), lambda: self.five(t - 3))
+        when((t >= 2) & (t - 2 < self.count), lambda: self.four(t - 2))
+        when((t >= 1) & (t - 1 < self.count), lambda: self.three(t - 1))
+
+    def finish(self):
+        for stage in (2, 3, 4):
+            for cp in self.copies(stage, self.count - 1):
+                cp.wait_send()
+
+
+def mlp_kernel(tok, gout, attnT, mod, bias, bup, wall, bo, dx1, dat, dob, gm, dmod_ref, db_ref, dbup_ref,
+               h2, hT, dzb, dzT, hS, zS, z, dh2, o_s, wout, wbuf, ad, adS, wsem, wosem, osem, xs, xr, ps, pr, pc, *sc):
+    at = Place()
+    at.greet()
+    pair = Pair(at, ad, adS, ps, pr, pc, NJ)
+    scatter = Scatter(at, sc, gm, NJ)
+
+    def fetch(j, slot):
+        return pltpu.make_async_copy(wall.at[4 + j], wbuf.at[slot], wsem.at[slot])
+
+    def co(g):
+        return pltpu.make_async_copy(wall.at[g, :, 768:1024], wout.at[:, g * 256 : (g + 1) * 256], wosem.at[g])
+
+    for g in range(4):
+        co(g).start()
+    fetch(0, 0).start()
+    gate1, shift2, scale2, gate2 = mod[2:3], mod[3:4], mod[4:5], mod[5:6]
+    db_ref[...] = jnp.zeros_like(db_ref)
+    dmod_ref[...] = jnp.zeros_like(dmod_ref)
+    for g in range(4):
+        co(g).wait()
+
+    def pre(r):
+        o = dot(attnT[:, r], wout[...], TN) + bias[2:3]
+        o_s[r, :] = o
+        x1 = tok[r, :].astype(f32) + gate1 * o
+        xh, _ = nrm(x1)
+        h2[r, :] = (xh * (1.0 + scale2) + shift2).astype(bf)
+        dz = gout[r, :].astype(f32) * gate2
+        dzb[r, :] = dz.astype(bf)
+        db_ref[3:4] += jnp.sum(dz, axis=0, keepdims=True)
+
+    rows_loop(S, 256, pre)
+    for i in range(4):
+        r = slice(i * 256, (i + 1) * 256)
+        hT[:, :, :, r] = h2[r, :].T.reshape(16, 2, 32, 256)
+        dzT[:, :, :, r] = dzb[r, :].T.reshape(16, 2, 32, 256)
+    halves = [
+        remote(hT.at[:, 1 - at.c], hS, xs.at[0], xr.at[0], at.to_c),
+        remote(dzT.at[:, 1 - at.c], zS, xs.at[1], xr.at[1], at.to_c),
+    ]
+    for cp in halves:
+        cp.start()
+    z[...] = jnp.zeros_like(z)
+    dh2[...] = jnp.zeros_like(dh2)
+
+    def chunk(j, _):
+        def forward():
+            slot = lax.rem(j, 2)
+            when(j + 1 < NJ, lambda: fetch(j + 1, 1 - slot).start())
+            fetch(j, slot).wait()
+            pair.reuse(j)
+            dbup_ref[j] = jnp.zeros((1, CH), f32)
+
+            def row(r):
+                u = dot(h2[r, :], wbuf[slot, :, :CH]) + bup[j]
+                a, sl = gelu_pair(u)
+                ab = a.astype(bf)
+                ad[slot, r, CH:] = ab
+                d = dot(dzb[r, :], wbuf[slot, :, CH:]) * sl
+                dbup_ref[j] += jnp.sum(d, axis=0, keepdims=True)
+                db_ = d.astype(bf)
+                ad[slot, r, :CH] = db_
+                z[r, :] += dot(ab, wbuf[slot, :, CH:], NT)
+                dh2[r, :] += dot(db_, wbuf[slot, :, :CH], NT)
+
+            rows_loop(S, 512, row)
+            pair.start(j)
+
+        when(j < NJ, forward)
+        scatter.tick(j - 1)
+
+        def weights():
+            i = j - 1
+            slot = lax.rem(i, 2)
+            when(j == 1, lambda: [cp.wait_recv() for cp in halves])
+            pair.arrived(i)
+            for q, (lhs, lhs_s) in enumerate(((hT, hS), (dzT, zS))):
+                cols = slice(q * CH, (q + 1) * CH)
+                t = dot(lhs[:, at.c].reshape(512, S), ad[slot, :, cols]) + dot(lhs_s[...].reshape(512, S), adS[slot, :, cols])
+                scatter.acc[:, :, :, :, cols] = t.reshape(4, 2, 2, 32, CH)
+            pair.free(i)
+            scatter.two(i)
+
+        when(j >= 1, weights)
+        return 0
+
+    lax.fori_loop(0, NJ + 1, chunk, 0)
+    pair.finish()
+    for cp in halves:
+        cp.wait_send()
+
+    def post(r):
+        g = gout[r, :].astype(f32)
+        o = o_s[r, :]
+        x1 = tok[r, :].astype(f32) + gate1 * o
+        xh, rstd = nrm(x1)
+        zz = z[r, :] + bias[3:4]
+        h2[r, :] = (x1 + gate2 * zz).astype(bf)
+        dmod_ref[5:6] += jnp.sum(g * zz, axis=0, keepdims=True)
+        dh = dh2[r, :]
+        dmod_ref[3:4] += jnp.sum(dh, axis=0, keepdims=True)
+        dmod_ref[4:5] += jnp.sum(dh * xh, axis=0, keepdims=True)
+        gg = dh * (1.0 + scale2)
+        dx = g + rstd * (gg - jnp.mean(gg, axis=-1, keepdims=True) - xh * jnp.mean(gg * xh, axis=-1, keepdims=True))
+        dh2[r, :] = dx
+        dmod_ref[2:3] += jnp.sum(dx * o, axis=0, keepdims=True)
+        do = dx * gate1
+        db_ref[2:3] += jnp.sum(do, axis=0, keepdims=True)
+        dob_ = do.astype(bf)
+        dzb[r, :] = dob_
+        ad[0, r, :] = dot(dob_, wout[...], NT).astype(bf)
+
+    def post_half(h):
+        def body(i, _):
+            post(pl.ds(pl.multiple_of(h * 512 + i * 128, 128), 128))
+            return 0
+
+        lax.fori_loop(0, 4, body, 0)
+
+    post_half(0)
+    scatter.tick(NJ)
+    post_half(1)
+    outs = [pltpu.make_async_copy(h2, bo, osem.at[0]), pltpu.make_async_copy(dh2, dx1, osem.at[1]), pltpu.make_async_copy(dzb, dob, osem.at[2])]
+    outs += [pltpu.make_async_copy(ad.at[0, :, g * 256 : (g + 1) * 256], dat.at[g], osem.at[3 + g]) for g in range(4)]
+    for cp in outs:
+        cp.start()
+    scatter.tick(NJ + 1)
+    scatter.tick(NJ + 2)
+    for cp in outs:
+        cp.wait()
+    scatter.finish()
+
+
+def mlp(*a):
+    dma = pltpu.SemaphoreType.DMA
+    return pl.pallas_call(
+        mlp_kernel,
+        out_shape=(sd((S, D), bf), sd((S, D), f32), sd((4, S, 256), bf), sd((S, D), bf), sd((NJ, 32, 1024), f32), sd((8, D), f32), sd((8, D), f32), sd((NJ, 1, CH), f32)),
+        in_specs=[V] * 6 + [A],
+        out_specs=[A] * 4 + [V] * 4,
+        scratch_shapes=[pltpu.VMEM((S, D), bf), pltpu.VMEM((16, 2, 32, S), bf)] * 2
+        + [pltpu.VMEM((16, 32, S), bf)] * 2
+        + [pltpu.VMEM((S, D), f32)] * 3
+        + [pltpu.VMEM((D, D), bf), pltpu.VMEM((2, D, 2 * CH), bf), pltpu.VMEM((2, S, 2 * CH), bf), pltpu.VMEM((2, S, 2 * CH), bf)]
+        + [dma((2,)), dma((4,)), dma((7,)), dma((2,)), dma((2,)), dma((2,)), dma((2,)), pltpu.SemaphoreType.REGULAR]
+        + Scatter.shapes,
+        compiler_params=pltpu.CompilerParams(collective_id=4, has_side_effects=True, vmem_limit_bytes=63 * 2**20),
+        name="mlp",
+    )(*a)
+
+
+def back_kernel(tok, mod, qkv, dat, lse, dx1, h1T, attnT, dob, wall, ig, gq, dmod, dbq,
+                dk_s, dv_s, dqT_s, dh1, wbuf, ex, exS, hS, aS, wsem, xs, xr, ps, pr, pc, *sc):
+    c = LOG2E / 8.0
+    at = Place()
+    at.greet()
+    pair = Pair(at, ex, exS, ps, pr, pc, 4)
+    scatter = Scatter(at, sc, gq, 4)
+    halves = [
+        remote(h1T.at[:, 1 - at.c], hS, xs.at[0], xr.at[0], at.to_c),
+        remote(attnT.at[:, 1 - at.c], aS, xs.at[1], xr.at[1], at.to_c),
+    ]
+    for cp in halves:
+        cp.start()
+
+    def cp_w(g, slot):
+        return pltpu.make_async_copy(wall.at[g, :, 0:768], wbuf.at[slot], wsem.at[slot])
+
+    cp_w(0, 0).start()
+    dh1[...] = jnp.zeros_like(dh1)
+    dmod[...] = jnp.zeros_like(dmod)
+    dbq[...] = jnp.zeros_like(dbq)
+
+    def group(g, _):
+        slot = lax.rem(g, 2)
+        when(g < 3, lambda: cp_w(g + 1, 1 - slot).start())
+        pair.reuse(g)
+        ex[slot, :, 768:] = dob[:, pl.ds(pl.multiple_of(g * 256, 256), 256)]
+        for p in range(2):
+            sl = slice(p * 128, (p + 1) * 128)
+            slk = slice(256 + p * 128, 256 + (p + 1) * 128)
+            slv = slice(512 + p * 128, 512 + (p + 1) * 128)
+            kp, vp, q, da = qkv[g, :, slk], qkv[g, :, slv], qkv[g, :, sl], dat[g, :, sl]
+            kT = kp.T
+            for h in range(2):
+                s = dot(lane_half(kp, h), q, NT)
+                pT = jnp.exp2(s * c - lse[g, p * 2 + h : p * 2 + h + 1, :] * LOG2E)
+                dp = dot(lane_half(vp, h), da, NT)
+                delta = jnp.sum(pT * dp, axis=0, keepdims=True)
+                ds = (pT * (dp - delta)).astype(bf)
+                dv = dot(pT.astype(bf), lane_half(da, h))
+                dk = dot(ds, lane_half(q, h))
+                if h == 0:
+                    dv_s[...] = dv
+                    dk_s[...] = dk
+                else:
+                    dv_s[...] += dv
+                    dk_s[...] += dk
+                dqT_s[h * 64 : (h + 1) * 64, :] = dot(kT[h * 64 : (h + 1) * 64], ds)
+            dq = dqT_s[...].T * 0.125
+            dbq[g, :, sl] = jnp.sum(dq, axis=0, keepdims=True)
+            ex[slot, :, sl] = dq.astype(bf)
+            ex[slot, :, slk] = (dk_s[...] * 0.125).astype(bf)
+            dbq[g, :, slv] = jnp.sum(dv_s[...], axis=0, keepdims=True)
+            ex[slot, :, slv] = dv_s[...].astype(bf)
+        pair.start(g)
+        cp_w(g, slot).wait()
+
+        def wrow(r):
+            dh1[r, :] += dot(ex[slot, r, :768], wbuf[slot], NT)
+
+        rows_loop(D, 256, wrow)
+        scatter.tick(g)
+        when(g == 0, lambda: [cp.wait_recv() for cp in halves])
+        pair.arrived(g)
+        for lhs, lhs_s, cols in ((h1T, hS, slice(0, 768)), (attnT, aS, slice(768, 1024))):
+            t = dot(lhs[:, at.c].reshape(512, S), ex[slot, :, cols]) + dot(lhs_s[...].reshape(512, S), exS[slot, :, cols])
+            scatter.acc[:, :, :, :, cols] = t.reshape(4, 2, 2, 32, cols.stop - cols.start)
+        pair.free(g)
+        scatter.two(g)
+        return 0
+
+    lax.fori_loop(0, 4, group, 0)
+    pair.finish()
+    for cp in halves:
+        cp.wait_send()
+    scale1 = mod[1:2]
+
+    def post(r):
+        xh, rstd = nrm(tok[r, :].astype(f32))
+        dh = dh1[r, :]
+        dmod[0:1] += jnp.sum(dh, axis=0, keepdims=True)
+        dmod[1:2] += jnp.sum(dh * xh, axis=0, keepdims=True)
+        gg = dh * (1.0 + scale1)
+        ig[r, :] = dx1[r, :] + rstd * (gg - jnp.mean(gg, axis=-1, keepdims=True) - xh * jnp.mean(gg * xh, axis=-1, keepdims=True))
+
+    rows_loop(S, 128, post)
+    for t in (4, 5, 6):
+        scatter.tick(t)
+    scatter.finish()
+
+
+def back(*a):
+    dma = pltpu.SemaphoreType.DMA
+    return pl.pallas_call(
+        back_kernel,
+        out_shape=(sd((S, D), f32), sd((4, 32, 1024), f32), sd((8, D), f32), sd((4, 1, 768), f32)),
+        in_specs=[V] * 9 + [A],
+        out_specs=[V] * 4,
+        scratch_shapes=[pltpu.VMEM((S, 128), f32), pltpu.VMEM((S, 128), f32), pltpu.VMEM((128, S), f32), pltpu.VMEM((S, D), f32), pltpu.VMEM((2, D, 768), bf)]
+        + [pltpu.VMEM((2, S, 1024), bf)] * 2
+        + [pltpu.VMEM((16, 32, S), bf)] * 2
+        + [dma((2,)), dma((2,)), dma((2,)), dma((2,)), dma((2,)), pltpu.SemaphoreType.REGULAR]
+        + Scatter.shapes,
+        compiler_params=pltpu.CompilerParams(collective_id=5, has_side_effects=True, vmem_limit_bytes=63 * 2**20),
+        name="back",
+    )(*a)
+
 
 def adam_step(param, grad, first, second, decay):
     new_first = beta_first * first + (1.0 - beta_first) * grad
@@ -597,12 +1010,22 @@
         wall = lax.all_gather(mine, "dp", axis=1, tiled=True).reshape(12, 4, 2, 2, 2, 32, 1024)
         qkv, attn_t, lse, h1t = ka(False, tok, mod, bqkv, wall)
     wall = wall.reshape(12, D, 1024)
-    bo, dx1, dat, dw_mlp, dw_out, dmod_b, db, db_up = kb(512, tok, gout, attn_t, mod, brows, bup, wall)
-    ig, dw_qkv, dmod_a, db_qkv = kc(1024, tok, mod, qkv, dat, lse, dx1, h1t, wall)
+    if chips:
+        bo, dx1, dat, dob, g_mlp, dmod_b, db, db_up = mlp(tok, gout, attn_t, mod, brows, bup, wall)
+        parts = (16, 2, 32, S)
+        ig, g_qkvo, dmod_a, db_qkv = back(tok, mod, qkv, dat, lse, dx1, h1t.reshape(parts), attn_t.reshape(parts), dob, wall)
+        g_mlp = g_mlp.reshape(NJ, rows, 2, CH).transpose(1, 2, 0, 3).reshape(rows, 2 * FF)
+        g_qkvo = g_qkvo.reshape(4, rows, 4, 256).transpose(1, 2, 0, 3).reshape(rows, 4 * D)
+    else:
+        bo, dx1, dat, dw_mlp, dw_out, dmod_b, db, db_up = kb(512, tok, gout, attn_t, mod, brows, bup, wall)
+        ig, dw_qkv, dmod_a, db_qkv = kc(1024, tok, mod, qkv, dat, lse, dx1, h1t, wall)
+        g_mlp = lax.psum_scatter(dw_mlp, "dp", scatter_dimension=2, tiled=True)
+        g_out = lax.psum_scatter(dw_out, "dp", scatter_dimension=0, tiled=True)
+        g_qkv = lax.psum_scatter(dw_qkv, "dp", scatter_dimension=1, tiled=True)
+        g_qkv = g_qkv.reshape(4, rows, 3, 256).transpose(1, 2, 0, 3).reshape(rows, 3 * D)
+        g_qkvo = jnp.concatenate([g_qkv, g_out], axis=1)
+        g_mlp = g_mlp.transpose(2, 1, 0, 3).reshape(rows, 2 * FF)
     dmod = (dmod_a + dmod_b)[:6].reshape(1, 6 * D)
-    g_mlp = lax.psum_scatter(dw_mlp, "dp", scatter_dimension=2, tiled=True)
-    g_out = lax.psum_scatter(dw_out, "dp", scatter_dimension=0, tiled=True)
-    g_qkv = lax.psum_scatter(dw_qkv, "dp", scatter_dimension=1, tiled=True)
     db_qkv = db_qkv.reshape(4, 3, 256).transpose(1, 0, 2).reshape(3, D)
     bias_row = jnp.concatenate([db_qkv[0], db_qkv[2], db[2], db_up.reshape(FF), db[3], dmod[0]])
     dmod_bf = dmod.astype(bf)
@@ -623,9 +1046,7 @@
         cond_grad = lax.all_to_all(cond_part, "dp", split_axis=0, concat_axis=1, tiled=True)
     sigma = jax.nn.sigmoid(condition)
     cond_grad = cond_grad * (sigma * (1.0 + condition * (1.0 - sigma)))
-    g_qkv = g_qkv.reshape(4, rows, 3, 256).transpose(1, 2, 0, 3).reshape(rows, 3 * D)
-    g_mlp = g_mlp.transpose(2, 1, 0, 3).reshape(rows, 2 * FF)
-    weight_grad = jnp.concatenate([g_qkv, g_out, g_mlp, g_ada], axis=1)
+    weight_grad = jnp.concatenate([g_qkvo, g_mlp, g_ada], axis=1)
     new_weights, new_first, new_second = adam_step(weights, weight_grad, first_moment, second_moment, weight_decay)
     new_biases, new_bias_first, new_bias_second = adam_step(biases, bias_grad, bias_first, bias_second, 0.0)
     return (bo[None], ig[None], cond_grad, weight_grad, bias_grad, new_weights, new_biases, new_first, new_second, new_bias_first, new_bias_second)

time: 1040 us -> 463 us (0.45)
  waiting for transfers between devices: 619 us -> 0 us
  Pallas kernels: 373 us -> 419 us
  between operations: 14.6 us -> 1.53 us
    reduce_scatter x3 -> x0, waiting for transfers between devices: 618 us -> none  [the longest x1 353 us: on_device(): g_mlp = lax.psum_scatter(dw_mlp, 'dp', scatter_dimension=2, tiled=True)]
    pallas_call x2, Pallas kernels: 172 us -> 220 us  [the longest x1 118 us: mlp(): pl.pallas_call(mlp_kernel, out_shape=(sd((S, D), bf), sd((S, D), f32), sd...]
  transfers between devices with their start and end apart: 3 -> 0, of which waited for: 3 -> 0; matrix products, arithmetic and copies ran while one was open for 1% -> 0% of each run, Pallas kernels for 3% -> 0%
where the time goes in v3:
time: 463 us; the launch traced here: 454 us
  Pallas kernels  419 us (90%)
  local copies, waits for them, and re-layouts  16.8 us (4%)
  other arithmetic  13.6 us (3%)
    pallas_call x1, Pallas kernels, ka(): pl.pallas_call(functools.partial(ka_kernel, comm), out_shape=out, in_spec...  143 us
    pallas_call x1, Pallas kernels, mlp(): pl.pallas_call(mlp_kernel, out_shape=(sd((S, D), bf), sd((S, D), f32), sd...  118 us
    pallas_call x1, Pallas kernels, back(): pl.pallas_call(back_kernel, out_shape=(sd((S, D), f32), sd((4, 32, 1024),...  103 us
    pallas_call x1, Pallas kernels, first(): pl.pallas_call(functools.partial(first_kernel, n, rows), out_shape=(sd((1...  27.1 us
    pallas_call x1, Pallas kernels, last(): pl.pallas_call(functools.partial(last_kernel, n), out_shape=(sd((8, 128),...  19.2 us
    pallas_call x1, Pallas kernels, swap(): pl.pallas_call(functools.partial(swap_kernel, n), out_shape=sd(cp.shape,...  9.36 us

profile of v3, /device:TPU:0, one launch (start us, length us, event | category | flops | bytes accessed | tf_op | source)
XLA Modules:
  0.0 453.6 jit_solution(15775436079471598901)
XLA Ops:
  0.8 0.7 reduce_precision.3
  1.5 0.7 convert_convert_fusion
  2.2 0.1 concatenate.16
  2.3 1.8 convert_element_type.25
  4.1 0.2 reshape.131
  4.3 0.1 copy.53
  4.4 0.2 reshape.132
  4.6 27.1 %first.1 = (f32[1,6144]{1,0:T(1,128)S(1)}, f32[32,16,128]{2,1,0:T(8,128)S(1)}) custom-call(f32[16,128]{1,0:T(8,128)S(1)} %bitcast.62, bf16[32,6144]{1,0:T(8,128)(2,1)S(1)} %slice.88.ada), custom_call_target="tpu_custom_call" | custom-call | tf_op jit(solution)/shard_map/first/pallas_call | solution.py:82
  31.8 0.1 reshape.128
  32.0 0.6 concatenate.17.mod
  32.6 0.7 maximum_maximum_fusion.bias
  33.3 0.1 slice.78
  33.4 0.6 slice.97.bup
  34.0 0.1 slice.71
  34.2 0.6 copy.28.bqkv
  34.9 0.2 copy.33
  35.0 0.4 copy.52
  35.5 0.4 reshape.134
  35.8 0.9 pad_maximum_fusion.1.w_in
  36.8 142.9 %attention_forward.1 = (bf16[4,1024,768]{2,1,0:T(8,128)(2,1)}, bf16[1024,1024]{1,0:T(8,128)(2,1)}, f32[4,4,1024]{2,1,0:T(4,128)}, bf16[1024,1024]{1,0:T(8,128)(2,1)}, bf16[12,4,2,2,2,32,1024]{6,5,4,3,2,1,0:T(8,128)(2,1)}) custom-call(bf16[1024,1024]{1,0:T(8,128)(2,1)} %bitcast.65, f32[8,1024]{1,0:T(8,128)} %concatenate.17.mod, f32[4,1,768]{2,1,0:T(1,128)} %copy.28.bqkv, ...), custom_call_target="tpu_custom_call" | custom-call | tf_op jit(solution)/shard_map/attention_forward/pallas_call | solution.py:481
  179.7 117.6 %mlp.1 = (bf16[1024,1024]{1,0:T(8,128)(2,1)}, f32[1024,1024]{1,0:T(8,128)}, bf16[4,1024,256]{2,1,0:T(8,128)(2,1)}, bf16[1024,1024]{1,0:T(8,128)(2,1)}, f32[8,32,...) custom-call(bf16[1024,1024]{1,0:T(8,128)(2,1)} %bitcast.66, ...), custom_call_target="tpu_custom_call" | custom-call | tf_op jit(solution)/shard_map/mlp/pallas_call | solution.py:845
  297.4 102.8 %back.1 = (f32[1024,1024]{1,0:T(8,128)}, f32[4,32,1024]{2,1,0:T(8,128)}, f32[8,1024]{1,0:T(8,128)}, f32[4,1,768]{2,1,0:T(1,128)}) custom-call(bf16[1024,1024]{1,0:T(8,128)(2,1)} %bitcast.67, f32[8,1024]{1,0:T(8,128)} %concatenate.17.mod, bf16[4,1024,768]{2,1,0:T(8,128)(2,1)} %get-tuple-element.37.qkv, bf16[4,1024,256]{2,1,0:T(8,128)(2,1)} %get-tuple-element.38.dat, ...), custom_call_target="tpu_custom_call" | custom-call | tf_op jit(solution)/shard_map/back/pallas_call | solution.py:954
  400.2 0.8 fusion.16
  401.1 0.7 copy.29
  401.8 0.8 fusion.13
  402.6 0.6 convert_element_type.27.dm
  403.3 0.1 reshape.140
  403.4 0.7 copy.36
  404.1 19.2 %last.1 = (f32[8,128]{1,0:T(8,128)}, bf16[32,48,128]{2,1,0:T(8,128)(2,1)}) custom-call(f32[32,8,128]{2,1,0:T(8,128)} %bitcast.84, bf16[48,128]{1,0:T(8,128)(2,1)} %convert_element_type.27.dm), custom_call_target="tpu_custom_call" | custom-call | tf_op jit(solution)/shard_map/last/pallas_call | solution.py:106
  423.3 1.4 fusion.3
  424.7 0.6 pad.10
  425.3 9.4 %swap.1 = f32[32,1,128]{2,1,0:T(1,128)} custom-call(f32[32,1,128]{2,1,0:T(1,128)} %bitcast.91), custom_call_target="tpu_custom_call" | custom-call | tf_op jit(solution)/shard_map/swap/pallas_call | solution.py:126
  434.6 0.8 slice_reduce_fusion
  435.4 0.1 reshape_squeeze.3
  435.5 0.6 multiply_multiply_fusion.1
  436.1 1.3 multiply_subtract_fusion.1
  437.4 1.3 fusion.1
  438.8 0.2 reshape.144
  439.0 0.3 copy.30
  439.4 0.3 reshape.145
  439.7 0.9 reshape.146
  440.6 0.6 copy.31
  441.2 0.6 copy.38
  441.8 0.4 copy-done
  442.2 6.0 %multiply_subtract_fusion = (f32[32,18432]{1,0:T(8,128)}, f32[32,18432]{1,0:T(8,128)}, f32[32,18432]{1,0:T(8,128)}, f32[32,18432]{1,0:T(8,128)}) fusion(f32[32,18432]{1,0:T(8,128)S(1)} %copy-done, f32[32,18432]{1,0:T(8,128)} %param.14, f32[32,18432]{1,0:T(8,128)} %param.15, f32[32,6144]{1,0:T(8,128)S(1)} %fusion.1, f32[32,8192]{1,0:T(8,128)S(1)} %bitcast.69, ...), kind=kLoop, calls=%fused_computation.3 | loop fusion | flops 9437184 | bytes 18874368 | tf_op jit(solution)/shard_map/sub | solution.py:974
  448.2 1.3 copy.63
  449.6 1.6 copy-done.2
  451.2 2.0 copy.64
  (52 shorter events, 0.6 us)
Async XLA Ops:
  4.1 30.8 %copy-start.1 = (bf16[32,18432]{1,0:T(8,128)(2,1)}, bf16[32,18432]{1,0:T(8,128)(2,1)S(1)}, u32[]{:S(2)}) copy-start(bf16[32,18432]{1,0:T(8,128)(2,1)S(1)} %convert_element_type.25) | copy-start | bytes 3538948
  297.3 104.5 %copy-start.6 = (f32[8,1024]{1,0:T(8,128)S(1)}, f32[8,1024]{1,0:T(8,128)}, u32[]{:S(2)}) copy-start(f32[8,1024]{1,0:T(8,128)} %get-tuple-element.48) | copy-start | bytes 98308
  297.3 105.9 %copy-start.7 = (f32[8,1,512]{2,1,0:T(1,128)S(1)}, f32[8,1,512]{2,1,0:T(1,128)}, u32[]{:S(2)}) copy-start(f32[8,1,512]{2,1,0:T(1,128)} %get-tuple-element.46) | copy-start | bytes 49156
  297.4 138.1 %copy-start.8 = (f32[1,1024]{1,0:T(1,128)S(1)}, f32[1,1024]{1,0:T(1,128)}, u32[]{:S(2)}) copy-start(f32[1,1024]{1,0:T(1,128)} %param.10) | copy-start | bytes 12292
  297.4 138.7 %copy-start.9 = (f32[448]{0:T(512)S(1)}, f32[448]{0:T(512)}, u32[]{:S(2)}) copy-start(f32[448]{0:T(512)} %param.13) | copy-start | bytes 5380
  297.4 138.7 %copy-start.10 = (f32[448]{0:T(512)S(1)}, f32[448]{0:T(512)}, u32[]{:S(2)}) copy-start(f32[448]{0:T(512)} %param.16) | copy-start | bytes 5380
  297.4 138.7 %copy-start.11 = (f32[448]{0:T(512)S(1)}, f32[448]{0:T(512)}, u32[]{:S(2)}) copy-start(f32[448]{0:T(512)} %param.17) | copy-start | bytes 5380
  400.2 38.5 %copy-start.5 = (f32[4,32,1024]{2,1,0:T(8,128)S(1)}, f32[4,32,1024]{2,1,0:T(8,128)}, u32[]{:S(2)}) copy-start(f32[4,32,1024]{2,1,0:T(8,128)} %get-tuple-element.50) | copy-start | bytes 1572868
  424.6 15.0 %copy-start.4 = (f32[8,32,1024]{2,1,0:T(8,128)S(1)}, f32[8,32,1024]{2,1,0:T(8,128)}, u32[]{:S(2)}) copy-start(f32[8,32,1024]{2,1,0:T(8,128)} %get-tuple-element.51) | copy-start | bytes 3145732
  440.6 1.7 copy-start
  442.2 6.0 %copy-start.3 = (bf16[1024,1024]{1,0:T(8,128)(2,1)S(1)}, bf16[1024,1024]{1,0:T(8,128)(2,1)}, u32[]{:S(2)}) copy-start(bf16[1024,1024]{1,0:T(8,128)(2,1)} %get-tuple-element.36) | copy-start | bytes 6291460
  448.2 2.9 copy-start.2
